TPU v7x, 32 devices: a whole 2x2x4 slice. The times are simulated.
32 devices in a mesh: grp: 2 (over x), rel: 16 (over z, y, core).
Axes of the slice: x: 2, y: 2, z: 4, core: 2. Of those that a mesh axis runs over, the one named last changes fastest.
Arguments:
- coarse: float32 [196608], P(('grp', 'rel')), parts along dimension 0, may hold values from -1 to 1
- background: float32 [4, 256, 256], P('grp'), parts along dimension 0, may hold values from 0 to 2
- sources: int32 [32], P(('grp', 'rel')), parts along dimension 0, may hold values from 0 to 131071, as said below
- durations: int32 [32], P(('grp', 'rel')), parts along dimension 0, may hold values from 1 to 6
- counts: int32 [32], P(('grp', 'rel')), parts along dimension 0, may hold values from 1 to 6
- sensors: int32 [32, 64], P(('grp', 'rel')), parts along dimension 0, may hold values from 0 to 131071, as said below
- observed: float32 [32, 64], P(('grp', 'rel')), parts along dimension 0, may hold values from -5 to 5
Outputs:
- direction: float32 [196608], P(('grp', 'rel')), parts along dimension 0
- misfit: float32 [32], P(('grp', 'rel')), parts along dimension 0
There are 2 independent parts, one for each index of `grp`. A program takes and returns all parts, laid end to end along the dimension named above; each array names one. Nothing has to cross between parts.
Inputs may be any that keep to these rules, and one draw needn't show every extreme that they name: `sources`: A flat cell index level * 256 * 256 + x * 256 + y. Flat cell indices like sources; half of a release's sensors lie within 3 cells horizontally of its source, on its level.
All inputs are finite; a program needn't handle non-finite values.
Results may differ from a plain program's by a relative error of at most 0.0003.
Values sent between devices are 32-bit elements; how exact they have to be, the bound alone decides.
No kernel may reach another device: no remote copies, remote signals or barrier semaphores. Data moves between devices by JAX's collectives and lax.ppermute only.
A program may use at most 64 MiB of HBM per device.

v0:
```python
import jax
import jax.numpy as jnp
from jax import lax
from jax.sharding import PartitionSpec as P

NX = 256
NY = 256
NZ = 2
STEPS = 6
NSENS = 64


def prolong(params):
    fields = params.reshape(3, NZ, NX // 2, NY // 2)
    fine = jnp.repeat(jnp.repeat(fields, 2, axis=2), 2, axis=3)
    diffusivity = 0.05 * jnp.exp(fine[0])
    wind_x = 0.08 * jnp.tanh(fine[1])
    wind_y = 0.08 * jnp.tanh(fine[2])
    return (diffusivity, wind_x, wind_y)


def advance(concentration, diffusivity, wind_x, wind_y, source, emission, live):
    padded = jnp.pad(concentration, 1)
    cell_west = padded[1:-1, :-2, 1:-1]
    cell_east = padded[1:-1, 2:, 1:-1]
    cell_south = padded[1:-1, 1:-1, :-2]
    cell_north = padded[1:-1, 1:-1, 2:]
    cell_below = padded[:-2, 1:-1, 1:-1]
    cell_above = padded[2:, 1:-1, 1:-1]
    spread = diffusivity * (
        cell_west
        + cell_east
        + cell_south
        + cell_north
        + cell_below
        + cell_above
        - 6.0 * concentration
    )
    carried = jnp.maximum(wind_x, 0.0) * (concentration - cell_west) + jnp.minimum(wind_x, 0.0) * (
        cell_east - concentration
    )
    carried = (
        carried
        + jnp.maximum(wind_y, 0.0) * (concentration - cell_south)
        + jnp.minimum(wind_y, 0.0) * (cell_north - concentration)
    )
    candidate = concentration + spread - carried
    candidate = candidate.reshape(-1).at[source].add(emission).reshape(concentration.shape)
    return jnp.where(live, candidate, concentration)


def release_loss(params, background, source, duration, count, sensor, observed):
    diffusivity, wind_x, wind_y = prolong(params)
    concentration = background
    for instant in range(STEPS):
        emission = 4.0 * jnp.logical_and(instant < duration, instant < count).astype(jnp.float32)
        concentration = advance(
            concentration, diffusivity, wind_x, wind_y, source, emission, instant < count
        )
    sampled = concentration.reshape(-1)[sensor]
    return 0.5 * jnp.sum((sampled - observed) ** 2)


def local(coarse, background, sources, durations, counts, sensors, observed):
    share = coarse.shape[0]
    whole = lax.all_gather(coarse, "rel", axis=0, tiled=True)

    def single(record):
        source, duration, count, sensor, watched = record
        value, pullback = jax.vjp(
            lambda params: release_loss(
                params, background, source, duration, count, sensor, watched
            ),
            whole,
        )
        (slope,) = pullback(jnp.ones_like(value))
        return (value / NSENS, slope)

    misfit, slopes = lax.map(single, (sources, durations, counts, sensors, observed))
    local_grad = jnp.sum(slopes, axis=0)
    gradient = lax.psum(local_grad, "rel")
    power = jnp.mean(gradient * gradient)
    own_part = lax.dynamic_slice_in_dim(gradient, lax.axis_index("rel") * share, share)
    direction = own_part / jnp.sqrt(power + 1e-06)
    return (direction, misfit)


def solution(mesh):
    in_specs = (
        P(("grp", "rel")),
        P("grp", None, None),
        P(("grp", "rel")),
        P(("grp", "rel")),
        P(("grp", "rel")),
        P(("grp", "rel"), None),
        P(("grp", "rel"), None),
    )
    out_specs = (P(("grp", "rel")), P(("grp", "rel")))
    return jax.shard_map(local, mesh=mesh, in_specs=in_specs, out_specs=out_specs, check_vma=False)
```

profile of v0, /device:TPU:0, one launch (start us, length us, event | category | flops | bytes accessed | tf_op | source)
XLA Modules:
  0.0 269.0 jit_solution(11481830166958399052)
XLA Ops:
  8.5 24.4 %all_gather.3 = f32[98304]{0:T(1024)S(1)} all-gather(f32[6144]{0:T(1024)} %param.19), channel_id=1, replica_groups=mesh['grp'=2,'rel'=16] {'rel'}, dimensions={0}, use_global_device_ids=true | all-gather | bytes 417792 | tf_op jit(solution)/shard_map/all_gather | solution.py:66
  49.6 2.0 reshape.467
  56.1 2.0 reshape.470
  62.8 2.0 reshape.473
  69.2 2.0 reshape.476
  73.6 2.1 gather_fusion
  78.0 2.1 broadcast_select_fusion.4
  80.0 2.0 select_n.248
  82.0 2.7 fusion.72
  84.7 2.0 select_n.256
  86.7 2.7 select_multiply_fusion.3
  101.0 1.7 copy.175
  102.7 2.0 broadcast_select_fusion.3
  104.7 2.0 copy.177
  106.7 1.7 broadcast.474
  112.8 1.7 copy.178
  114.5 2.0 broadcast_select_fusion.2
  116.5 2.1 copy.180
  118.6 1.7 broadcast_in_dim.122
  122.4 2.1 copy.212
  124.5 1.7 broadcast.477
  130.5 1.7 copy.213
  132.3 2.0 broadcast_select_fusion.1
  134.2 2.0 copy.215
  142.3 1.7 copy.216
  144.0 2.0 broadcast_select_fusion
  146.0 2.0 copy.218
  150.9 2.1 copy.230
  153.0 7.0 %multiply_bitcast_fusion.2 = (f32[1,2,256,256]{3,2,1,0:T(8,128)S(1)}, f32[2,256,256]{2,1,0:T(8,128)S(1)}) fusion(f32[2,256,256]{2,1,0:T(8,128)} %copy.212, f32[2,256,256]{2,1,0:T(8,128)} %copy.180, f32[2,256,256]{2,1,0:T(8,128)} %copy.177, f32[2,256,256]{2,1,0:T(8,128)} %select_n.248, f32[2,256,256]{2,1,0:T(8,128)} %copy-done.15, f32[2,256,256]{2,1,0:T(8,128)} %copy-done, ...), kind=kLoop, calls=%fused_computation.90 | loop fusion | flops 10616832 | bytes 13107205 | tf_op jit(solution)/shard_map/while/body/eval_jaxpr/transpose(jvp())/broadcast_in_dim | solution.py:18
  160.2 2.8 %multiply_bitcast_fusion = f32[1,2,256,256]{3,2,1,0:T(8,128)S(1)} fusion(f32[2,256,256]{2,1,0:T(8,128)S(1)} %copy.146, f32[2,256,256]{2,1,0:T(8,128)S(1)} %get-tuple-element.137, f32[2,256,256]{2,1,0:T(8,128)S(1)} %copy-done.8, f32[2,256,256]{2,1,0:T(8,128)S(1)} %copy-done.18, f32[2,256,256]{2,1,0:T(8,128)S(1)} %copy-done.7, ...), kind=kLoop, calls=%fused_computation.88 | loop fusion | flops 7733248 | bytes 7340036 | tf_op jit(solution)/shard_map/while/body/eval_jaxpr/transpose(jvp())/broadcast_in_dim | solution.py:16
  167.9 1.8 reduce_sum.46
  170.3 86.9 %all-reduce.41.cloned.1.call-done = f32[98304]{0:T(1024)} async-done(((f32[98304]{0:T(1024)}), f32[98304]{0:T(1024)}) %all-reduce.41.cloned.1.call-update) | async-done | bytes 393232 | tf_op jit(solution)/shard_map/psum | solution.py:81
  (136 shorter events, 73.2 us)
Async XLA Ops:
  7.2 250.1 %all-reduce.41.cloned.1.call-start = ((), (), s32[]{:S(2)}) async-start(), calls=%async_computation | async-start | bytes 786432 | tf_op jit(solution)/shard_map/psum | solution.py:81
  37.0 2.5 copy-start.11
  43.2 0.8 copy-start.2
  52.7 0.8 copy-start.13
  59.4 0.8 copy-start
  65.9 0.8 copy-start.15
  71.2 2.4 copy-start.23
  71.2 4.5 %copy-start.22 = (f32[1,64]{1,0:T(1,128)S(1)}, f32[1,64]{1,0:T(1,128)}, u32[]{:S(2)}) copy-start(f32[1,64]{1,0:T(1,128)} %param.25) | copy-start | bytes 772
  89.4 0.8 copy-start.9
  90.7 0.8 copy-start.4
  92.1 0.8 copy-start.6
  94.3 1.5 copy-start.17
  152.9 7.1 %copy-start.1 = (f32[2,256,256]{2,1,0:T(8,128)S(1)}, f32[2,256,256]{2,1,0:T(8,128)}, u32[]{:S(2)}) copy-start(f32[2,256,256]{2,1,0:T(8,128)} %copy-done) | copy-start | bytes 1572868
  152.9 7.1 %copy-start.3 = (f32[2,256,256]{2,1,0:T(8,128)S(1)}, f32[2,256,256]{2,1,0:T(8,128)}, u32[]{:S(2)}) copy-start(f32[2,256,256]{2,1,0:T(8,128)} %copy-done.2) | copy-start | bytes 1572868
  152.9 7.1 %copy-start.5 = (f32[2,256,256]{2,1,0:T(8,128)S(1)}, f32[2,256,256]{2,1,0:T(8,128)}, u32[]{:S(2)}) copy-start(f32[2,256,256]{2,1,0:T(8,128)} %copy-done.4) | copy-start | bytes 1572868
  152.9 7.1 %copy-start.7 = (f32[2,256,256]{2,1,0:T(8,128)S(1)}, f32[2,256,256]{2,1,0:T(8,128)}, u32[]{:S(2)}) copy-start(f32[2,256,256]{2,1,0:T(8,128)} %copy-done.6) | copy-start | bytes 1572868
  152.9 7.1 %copy-start.8 = (f32[2,256,256]{2,1,0:T(8,128)S(1)}, f32[2,256,256]{2,1,0:T(8,128)}, u32[]{:S(2)}) copy-start(f32[2,256,256]{2,1,0:T(8,128)} %select_n.248) | copy-start | bytes 1572868
  153.0 7.1 %copy-start.10 = (f32[2,256,256]{2,1,0:T(8,128)S(1)}, f32[2,256,256]{2,1,0:T(8,128)}, u32[]{:S(2)}) copy-start(f32[2,256,256]{2,1,0:T(8,128)} %copy-done.9) | copy-start | bytes 1572868
  153.0 7.1 %copy-start.12 = (f32[2,256,256]{2,1,0:T(8,128)S(1)}, f32[2,256,256]{2,1,0:T(8,128)}, u32[]{:S(2)}) copy-start(f32[2,256,256]{2,1,0:T(8,128)} %param.20) | copy-start | bytes 1572868
  153.0 7.1 %copy-start.14 = (f32[2,256,256]{2,1,0:T(8,128)S(1)}, f32[2,256,256]{2,1,0:T(8,128)}, u32[]{:S(2)}) copy-start(f32[2,256,256]{2,1,0:T(8,128)} %copy-done.13) | copy-start | bytes 1572868
  153.0 7.1 %copy-start.16 = (f32[2,256,256]{2,1,0:T(8,128)S(1)}, f32[2,256,256]{2,1,0:T(8,128)}, u32[]{:S(2)}) copy-start(f32[2,256,256]{2,1,0:T(8,128)} %copy-done.15) | copy-start | bytes 1572868
  153.0 7.1 %copy-start.18 = (f32[2,256,256]{2,1,0:T(8,128)S(1)}, f32[2,256,256]{2,1,0:T(8,128)}, u32[]{:S(2)}) copy-start(f32[2,256,256]{2,1,0:T(8,128)} %copy-done.17) | copy-start | bytes 1572868
  160.1 2.9 %copy-start.19 = (f32[2,256,256]{2,1,0:T(8,128)S(1)}, f32[2,256,256]{2,1,0:T(8,128)}, u32[]{:S(2)}) copy-start(f32[2,256,256]{2,1,0:T(8,128)} %copy.215) | copy-start | bytes 1572868
  160.1 2.9 %copy-start.20 = (f32[2,256,256]{2,1,0:T(8,128)S(1)}, f32[2,256,256]{2,1,0:T(8,128)}, u32[]{:S(2)}) copy-start(f32[2,256,256]{2,1,0:T(8,128)} %copy.218) | copy-start | bytes 1572868
  160.1 2.9 %copy-start.21 = (f32[2,256,256]{2,1,0:T(8,128)S(1)}, f32[2,256,256]{2,1,0:T(8,128)}, u32[]{:S(2)}) copy-start(f32[2,256,256]{2,1,0:T(8,128)} %copy.230) | copy-start | bytes 1572868
Sparse Core Ops, SparseCore 0:
  169.8 87.4 all-reduce.40
where the time goes:
time: 271 us; the launch traced here: 269 us
  waiting for transfers between devices  87 us (32%)
  local copies, waits for them, and re-layouts  79.9 us (29%)
  other arithmetic  58.6 us (22%)
  blocking collectives  24.4 us (9%)
  between operations  19.1 us (7%)
    psum x1, waiting for transfers between devices, local(): gradient = lax.psum(local_grad, 'rel')  86.9 us
    all_gather x1, blocking collectives, local(): whole = lax.all_gather(coarse, 'rel', axis=0, tiled=True)  24.4 us
    broadcast_in_dim x22, local copies, waits for them, and re-layouts, prolong(): fine = jnp.repeat(jnp.repeat(fields, 2, axis=2), 2, axis=3)  18.5 us
    reshape x6, local copies, waits for them, and re-layouts, advance(): candidate.reshape(-1).at[source].add(emission).reshape(concentration.shape)  9.79 us
    select_n x7, other arithmetic, advance(): return jnp.where(live, candidate, concentration)  9.15 us
    unnamed x55, local copies, waits for them, and re-layouts  8.68 us
    mul x5, other arithmetic, advance(): diffusivity * (cell_west + cell_east + cell_south + cell_north + cell_bel...  7.88 us
    broadcast_in_dim x1, other arithmetic, prolong(): wind_y = 0.08 * jnp.tanh(fine[2])  7.02 us
  transfers between devices with their start and end apart: 1, of which 1 were waited for; matrix products, arithmetic and copies ran while one was open for 0% of the time, Pallas kernels for 0%

commit v1 on v0

v1 whole, which is shorter than its diff:
```python
import functools

import jax
import jax.numpy as jnp
from jax import lax
from jax.experimental import pallas as pl
from jax.experimental.pallas import tpu as pltpu
from jax.sharding import PartitionSpec as P

STEPS = 6
NSENS = 64
PAD = 8
BATCH = 32
SLOTS = 16
ROWS = 128
LANES = 128
PLANE = ROWS + 2 * PAD
FIELD = 8 * PLANE
VMEM_LIMIT = 40 * 1024 * 1024
F32, BF16, I32 = jnp.float32, jnp.bfloat16, jnp.int32


def loop(first, end, unroll=1):
    def run(body):
        lax.fori_loop(first, end, body, None, unroll=unroll)

    return run


def plane_at(z, px, py):
    return ((z * 2 + px) * 2 + py) * PLANE + PAD


def split(value):
    high = value.astype(BF16)
    return high, (value - high.astype(F32)).astype(BF16)


def pack_kernel(coarse_ref, sensors_ref, observed_ref, source_ref, duration_ref, count_ref, out_ref):
    rows = coarse_ref.shape[0]
    out_ref[...] = jnp.zeros_like(out_ref)
    out_ref[pl.ds(0, rows), :] = coarse_ref[...]
    out_ref[pl.ds(rows, 1), pl.ds(0, NSENS)] = sensors_ref[...].astype(F32)
    out_ref[pl.ds(rows, 1), pl.ds(NSENS, NSENS)] = observed_ref[...]
    lane = lax.broadcasted_iota(I32, (1, LANES), 1)
    record = jnp.where(lane == 0, source_ref[0], jnp.where(lane == 1, duration_ref[0], count_ref[0]))
    out_ref[pl.ds(rows + 1, 1), :] = record.astype(F32)


def planes_kernel(background_ref, out_ref, half_ref):
    width = background_ref.shape[2]
    out_ref[...] = jnp.zeros_like(out_ref)
    column = lax.broadcasted_iota(I32, (width, width), 1)
    row = lax.broadcasted_iota(I32, (width, width), 0)
    wanted = jnp.where(column < LANES, 2 * column, 2 * (column - LANES) + 1)
    pick = (row == wanted).astype(F32)
    for z in range(2):
        sorted_lanes = jnp.dot(
            background_ref[z], pick, precision=lax.Precision.HIGHEST, preferred_element_type=F32
        )
        for py in range(2):
            half_ref[z * 2 + py] = sorted_lanes[:, py * LANES : (py + 1) * LANES]
            for px in range(2):
                out_ref[pl.ds(plane_at(z, px, py), ROWS), :] = half_ref[z * 2 + py, pl.ds(px, ROWS, stride=2), :]


def gradient_kernel(
    order,
    rows,
    first_ref,
    second_ref,
    planes_ref,
    direction_ref,
    misfit_ref,
    par,
    coef,
    hist,
    lam_a,
    lam_b,
    acc,
    grad,
    sens_rows,
    meta_rows,
    table,
    gathered,
    scattered,
    scalars,
    sem,
):
    blocks = len(order)
    block = first_ref.shape[0] // (blocks // 2)
    me = lax.axis_index("rel")
    groups = -(-blocks // SLOTS)
    lane = lax.broadcasted_iota(I32, (8, LANES), 1)
    sub = lax.broadcasted_iota(I32, (8, LANES), 0)

    par[pl.ds(0, 8), :] = jnp.zeros((8, LANES), F32)
    par[pl.ds(8 + 6 * ROWS, 8), :] = jnp.zeros((8, LANES), F32)
    for p in range(blocks):
        ref = first_ref if p < blocks // 2 else second_ref
        at = (p % (blocks // 2)) * block
        owner = me ^ order[p]
        if rows % 8 == 0:
            place = pl.multiple_of(owner * rows + 8, 8)
        else:
            place = owner * rows + 8
        par[pl.ds(place, rows), :] = ref[pl.ds(at, rows), :]
        sens_rows[pl.ds(owner, 1), :] = ref[pl.ds(at + rows, 1), :]
        meta_rows[pl.ds(owner, 1), :] = ref[pl.ds(at + rows + 1, 1), :]

    wide = lax.broadcasted_iota(I32, (blocks, LANES), 1)
    release = lax.broadcasted_iota(I32, (blocks, LANES), 0)
    sens = jnp.where(wide < NSENS, sens_rows[...], 0.0).astype(I32)
    meta = meta_rows[...].astype(I32)
    source = jnp.broadcast_to(meta[:, 0:1], (blocks, LANES))
    duration = jnp.broadcast_to(meta[:, 1:2], (blocks, LANES))
    count = jnp.broadcast_to(meta[:, 2:3], (blocks, LANES))
    fine_x, fine_y = (sens >> 8) & 255, sens & 255
    plane = (sens >> 16) * 4 + (fine_x & 1) * 2 + (fine_y & 1)
    cell_x, cell_y = fine_x >> 1, fine_y >> 1
    left_x = (((source >> 8) & 255) >> 1) - 3
    left_y = ((source & 255) >> 1) - 3
    off_x, off_y = cell_x - left_x, cell_y - left_y
    inside = (off_x >= 0) & (off_x < 8) & (off_y >= 0) & (off_y < 8)
    patch_row = jnp.where(inside, plane * 8 + off_x, -1)
    patch_lane = jnp.where(inside, (release % SLOTS) * 8 + off_y, -1)
    address = (count - 1) * FIELD + plane * PLANE + PAD + cell_x
    row_id = (plane * ROWS + cell_x).astype(F32)
    for at, value in ((0, source), (1, duration), (2, count), (3, left_x), (4, left_y)):
        address = jnp.where(wide == NSENS + at, value, address)
    table[...] = address
    copy = pltpu.make_async_copy(table, scalars, sem)
    copy.start()

    names = ("centre", "east", "west", "north", "south", "diff", "south0", "north1", "northr", "southl", "wx", "wy", "fx", "fy")
    index = {name: i for i, name in enumerate(names)}

    def coef_at(name, z, x):
        return pl.ds((index[name] * 2 + z) * PLANE + PAD + x, 8)

    zeros = jnp.zeros((8, LANES), F32)
    for z in range(2):
        coef[coef_at("east", z, -8), :] = zeros
        coef[coef_at("west", z, ROWS), :] = zeros

    def coefficients(p0, p1, p2):
        diff = 0.05 * jnp.exp(p0)
        t1, t2 = jnp.tanh(p1), jnp.tanh(p2)
        wx, wy = 0.08 * t1, 0.08 * t2
        east, west = diff - jnp.minimum(wx, 0.0), diff + jnp.maximum(wx, 0.0)
        north, south = diff - jnp.minimum(wy, 0.0), diff + jnp.maximum(wy, 0.0)
        centre = 1.0 - (east + west + north + south + 2.0 * diff)
        return dict(
            centre=centre, east=east, west=west, north=north, south=south, diff=diff,
            wx=wx, wy=wy, fx=0.08 * (1.0 - t1 * t1), fy=0.08 * (1.0 - t2 * t2),
        )

    @loop(0, ROWS // 8, unroll=4)
    def _(i, carry):
        x = pl.multiple_of(i * 8, 8)
        for z in range(2):
            p0, p1, p2 = (par[pl.ds((f * 2 + z) * ROWS + 8 + x, 8), :] for f in range(3))
            made = coefficients(p0, p1, p2)
            made["south0"] = jnp.where(lane == 0, 0.0, made["south"])
            made["north1"] = jnp.where(lane == LANES - 1, 0.0, made["north"])
            made["northr"] = jnp.where(lane == 0, 0.0, pltpu.roll(made["north"], 1, 1))
            made["southl"] = jnp.where(lane == LANES - 1, 0.0, pltpu.roll(made["south"], LANES - 1, 1))
            for name, value in made.items():
                coef[coef_at(name, z, x), :] = value
        return carry

    for p in range(8):
        for ref, fields in ((hist, STEPS), (lam_a, 1), (lam_b, 1)):
            for f in range(fields):
                ref[pl.ds(f * FIELD + p * PLANE, 8), :] = zeros
                ref[pl.ds(f * FIELD + p * PLANE + PAD + ROWS, 8), :] = zeros

    def load(ref, base, x):
        def at(z, px, py, shift=0):
            return ref[pl.ds(base + plane_at(z, px, py) + x + shift, 8), :]

        own = [[[at(z, px, py) for py in range(2)] for px in range(2)] for z in range(2)]
        odd = [[at(z, 1, py, -1) for py in range(2)] for z in range(2)]
        even = [[at(z, 0, py, 1) for py in range(2)] for z in range(2)]
        return own, odd, even

    def forward(src, src_base, dst, dst_base):
        @loop(0, ROWS // 8, unroll=2)
        def _(i, carry):
            x = pl.multiple_of(i * 8, 8)
            own, odd, even = load(src, src_base, x)
            for z in range(2):
                k = {
                    name: coef[coef_at(name, z, x), :]
                    for name in ("centre", "east", "west", "north", "south", "diff", "south0", "north1")
                }
                for px in range(2):
                    c0, c1 = own[z][px]
                    along_y = (
                        k["north"] * c1 + k["south0"] * pltpu.roll(c1, 1, 1),
                        k["north1"] * pltpu.roll(c0, LANES - 1, 1) + k["south"] * c0,
                    )
                    for py in range(2):
                        if px == 0:
                            along_x = k["east"] * own[z][1][py] + k["west"] * odd[z][py]
                        else:
                            along_x = k["east"] * even[z][py] + k["west"] * own[z][0][py]
                        new = (k["centre"] * own[z][px][py] + along_x) + (
                            along_y[py] + k["diff"] * own[1 - z][px][py]
                        )
                        dst[pl.ds(dst_base + plane_at(z, px, py) + x, 8), :] = new
            return carry

    forward(planes_ref, 0, hist, 0)
    for t in range(1, STEPS):
        forward(hist, (t - 1) * FIELD, hist, t * FIELD)

    copy.wait()

    @loop(0, blocks)
    def _(r, carry):
        to = pl.multiple_of(r * NSENS, NSENS)
        for s in range(NSENS):
            gathered[pl.ds(to + s, 1), :] = hist[pl.ds(scalars[r, s], 1), :]
        return carry

    slot = lane >> 3
    patches = []
    for g in range(groups):
        members = range(g * SLOTS, min(blocks, (g + 1) * SLOTS))
        pp = [[zeros, zeros] for _ in range(3)]
        at_x, at_y, of_plane, lasts, emits = (jnp.zeros((8, LANES), I32) for _ in range(5))
        for r in members:
            here = slot == r % SLOTS
            src, dur, cnt = scalars[r, NSENS], scalars[r, NSENS + 1], scalars[r, NSENS + 2]
            x0, y0 = scalars[r, NSENS + 3], scalars[r, NSENS + 4]
            shift = (8 * (r % SLOTS) - y0) & (LANES - 1)
            for f in range(3):
                for z in range(2):
                    window = par[pl.ds((f * 2 + z) * ROWS + 8 + x0, 8), :]
                    pp[f][z] = jnp.where(here, pltpu.roll(window, shift, 1), pp[f][z])
            src_plane = (src >> 16) * 4 + ((src >> 8) & 1) * 2 + (src & 1)
            at_x = jnp.where(here, x0, at_x)
            at_y = jnp.where(here, y0, at_y)
            of_plane = jnp.where(here, src_plane, of_plane)
            emits = jnp.where(here, dur, emits)
            lasts = jnp.where(here, cnt, lasts)
        in_x, in_y = at_x + sub, at_y + (lane & 7)
        valid = (in_x >= 0) & (in_x < ROWS) & (in_y >= 0) & (in_y < LANES)
        ks = []
        for z in range(2):
            made = coefficients(pp[0][z], pp[1][z], pp[2][z])
            ks.append({name: jnp.where(valid, value, 0.0) for name, value in made.items()})
        spot = (sub == 3) & ((lane & 7) == 3)
        state = [[[zeros for _ in range(2)] for _ in range(2)] for _ in range(2)]
        plume = []
        for t in range(STEPS):
            plume.append(state)
            new = [[[None, None], [None, None]], [[None, None], [None, None]]]
            for z in range(2):
                k = ks[z]
                for px in range(2):
                    for py in range(2):
                        c = state[z][px][py]
                        other_x, other_y = state[z][1 - px][py], state[z][px][1 - py]
                        if px == 0:
                            along_x = k["east"] * other_x + k["west"] * pltpu.roll(other_x, 1, 0)
                        else:
                            along_x = k["east"] * pltpu.roll(other_x, 7, 0) + k["west"] * other_x
                        if py == 0:
                            along_y = k["north"] * other_y + k["south"] * pltpu.roll(other_y, 1, 1)
                        else:
                            along_y = k["north"] * pltpu.roll(other_y, LANES - 1, 1) + k["south"] * other_y
                        value = (k["centre"] * c + along_x) + (along_y + k["diff"] * state[1 - z][px][py])
                        emit = spot & (of_plane == z * 4 + px * 2 + py) & (t < emits)
                        value = value + jnp.where(emit, 4.0, 0.0)
                        new[z][px][py] = jnp.where(t < lasts, value, c)
            state = new
        patches.append((ks, valid, lasts, plume, state))

    lane_f, row_f = patch_lane.astype(F32), patch_row.astype(F32)
    first_half = wide < NSENS
    turn_a = jnp.where(first_half, cell_y.astype(F32), pltpu.roll(lane_f, NSENS, 1)).T
    turn_b = jnp.where(first_half, row_f, pltpu.roll(row_id, NSENS, 1)).T
    turn_c = sens_rows[...].T
    lane64 = lax.broadcasted_iota(I32, (NSENS, LANES), 1).astype(F32)
    lane_sq = lax.broadcasted_iota(I32, (NSENS, NSENS), 1).astype(F32)
    sub_sq = lax.broadcasted_iota(I32, (NSENS, NSENS), 0).astype(F32)
    batch = (lane_sq.astype(I32) // BATCH) == (sub_sq.astype(I32) // BATCH)
    loss = jnp.zeros((NSENS, LANES), F32)
    seeds = []
    for g in range(groups):
        members = range(g * SLOTS, min(blocks, (g + 1) * SLOTS))
        final = patches[g][4]
        flat = jnp.concatenate([final[z][px][py] for z in range(2) for px in range(2) for py in range(2)], axis=0)
        flat = jnp.concatenate(split(flat), axis=1)
        seed = jnp.zeros((NSENS, 2 * LANES), F32)
        for r in members:
            def column(turned, half):
                return jnp.broadcast_to(turned[half * NSENS : (half + 1) * NSENS, r : r + 1], (NSENS, LANES))

            own_lane, own_patch = column(turn_a, 0), column(turn_a, 1)
            own_row, own_cell = column(turn_b, 0), column(turn_b, 1)
            watched = column(turn_c, 1)
            pick = (own_row[:, :NSENS] == lane_sq).astype(BF16)
            near = jnp.dot(pick, flat, preferred_element_type=F32)
            near = near[:, :LANES] + near[:, LANES:]
            on_lane, on_patch = lane64 == own_lane, lane64 == own_patch
            value = jnp.where(on_lane, gathered[pl.ds(r * NSENS, NSENS), :], 0.0)
            value = value + jnp.where(on_patch, near, 0.0)
            residual = jnp.sum(value, axis=1, keepdims=True) - watched
            loss = jnp.where(me == r, residual * residual, loss)
            same = own_cell[:, :NSENS] == jnp.broadcast_to(row_id[r : r + 1, :NSENS], (NSENS, NSENS))
            same = (same & batch).astype(BF16)
            spread = jnp.dot(
                same,
                jnp.concatenate(split(jnp.where(on_lane, residual, 0.0)), axis=1),
                preferred_element_type=F32,
            )
            scattered[pl.ds(r * NSENS, NSENS), :] = spread[:, :LANES] + spread[:, LANES:]
            put = (sub_sq == jnp.broadcast_to(row_f[r : r + 1, :NSENS], (NSENS, NSENS))).astype(BF16)
            seed = seed + jnp.dot(
                put,
                jnp.concatenate(split(jnp.where(on_patch, residual, 0.0)), axis=1),
                preferred_element_type=F32,
            )
        seed = seed[:, :LANES] + seed[:, LANES:]
        seeds.append(
            [[[seed[((z * 2 + px) * 2 + py) * 8 :][:8] for py in range(2)] for px in range(2)] for z in range(2)]
        )
    misfit_ref[0] = jnp.sum(loss[:, 0:1]) * (0.5 / NSENS)

    def seed_sensors(ref, t):
        @loop(0, blocks)
        def _(r, carry):
            @pl.when(scalars[r, NSENS + 2] == t)
            def _():
                at = pl.multiple_of(r * NSENS, NSENS)
                for part in range(0, NSENS, BATCH):
                    spots, news = [], []
                    for s in range(part, part + BATCH):
                        spot = pl.ds(scalars[r, s] - (t - 1) * FIELD, 1)
                        spots.append(spot)
                        news.append(ref[spot, :] + scattered[pl.ds(at + s, 1), :])
                    for spot, new in zip(spots, news):
                        ref[spot, :] = new

            return carry

    def acc_at(q, z, x):
        return pl.ds((q * 2 + z) * ROWS + x, 8)

    def backward(src, dst, conc, conc_base, first, last):
        @loop(0, ROWS // 8, unroll=2)
        def _(i, carry):
            x = pl.multiple_of(i * 8, 8)
            lam, lam_odd, lam_even = load(src, 0, x)
            own, odd, even = load(conc, conc_base, x)
            diffs = [coef[coef_at("diff", z, x), :] for z in range(2)]
            for z in range(2):
                if not last:
                    k = {
                        name: coef[coef_at(name, z, x), :]
                        for name in ("centre", "east", "west", "north", "south", "northr", "southl")
                    }
                    east_m, west_p = coef[coef_at("east", z, x - 1), :], coef[coef_at("west", z, x + 1), :]
                    for px in range(2):
                        l0, l1 = lam[z][px]
                        along_y = (
                            k["south"] * l1 + k["northr"] * pltpu.roll(l1, 1, 1),
                            k["southl"] * pltpu.roll(l0, LANES - 1, 1) + k["north"] * l0,
                        )
                        for py in range(2):
                            if px == 0:
                                along_x = k["west"] * lam[z][1][py] + east_m * lam_odd[z][py]
                            else:
                                along_x = west_p * lam_even[z][py] + k["east"] * lam[z][0][py]
                            new = (k["centre"] * lam[z][px][py] + along_x) + (
                                along_y[py] + diffs[1 - z] * lam[1 - z][px][py]
                            )
                            dst[pl.ds(plane_at(z, px, py) + x, 8), :] = new
                sums = [None] * 5
                for px in range(2):
                    c0, c1 = own[z][px]
                    mid = c1 - c0
                    to_north = (mid, jnp.where(lane == LANES - 1, 0.0, pltpu.roll(c0, LANES - 1, 1)) - c1)
                    to_south = (c0 - jnp.where(lane == 0, 0.0, pltpu.roll(c1, 1, 1)), mid)
                    for py in range(2):
                        c, l = own[z][px][py], lam[z][px][py]
                        mid_x = own[z][1][py] - own[z][0][py]
                        if px == 0:
                            to_east, to_west = mid_x, c - odd[z][py]
                        else:
                            to_east, to_west = even[z][py] - c, mid_x
                        rise = own[1 - z][px][py] - 2.0 * c
                        for q, d in enumerate((to_east, to_west, to_north[py], to_south[py], rise)):
                            term = l * d
                            sums[q] = term if sums[q] is None else sums[q] + term
                for q in range(5):
                    at = acc_at(q, z, x)
                    acc[at, :] = sums[q] if first else acc[at, :] + sums[q]
            return carry

    @loop(0, FIELD // 64)
    def _(i, carry):
        lam_a[pl.ds(pl.multiple_of(i * 64, 64), 64), :] = jnp.zeros((64, LANES), F32)
        return carry

    src, dst = lam_a, lam_b
    for t in range(STEPS - 1, -1, -1):
        seed_sensors(src, t + 1)
        if t == 0:
            backward(src, dst, planes_ref, 0, False, True)
        else:
            backward(src, dst, hist, (t - 1) * FIELD, t == STEPS - 1, False)
        src, dst = dst, src

    def chain(sums, diff, wx, wy, fx, fy):
        to_east, to_west, to_north, to_south, rise = sums

        def wind(w, up, down, factor):
            plus = jnp.where(w > 0.0, 1.0, jnp.where(w == 0.0, 0.5, 0.0))
            return -(plus * up + (1.0 - plus) * down) * factor

        g0 = (to_east - to_west + to_north - to_south + rise) * diff
        return g0, wind(wx, to_west, to_east, fx), wind(wy, to_south, to_north, fy)

    @loop(0, ROWS // 8, unroll=2)
    def _(i, carry):
        x = pl.multiple_of(i * 8, 8)
        for z in range(2):
            sums = [acc[acc_at(q, z, x), :] for q in range(5)]
            made = chain(sums, *(coef[coef_at(name, z, x), :] for name in ("diff", "wx", "wy", "fx", "fy")))
            for f in range(3):
                grad[pl.ds((f * 2 + z) * ROWS + 8 + x, 8), :] = made[f]
        return carry

    for g in range(groups):
        members = range(g * SLOTS, min(blocks, (g + 1) * SLOTS))
        ks, valid, lasts, plume, _ = patches[g]
        seed = seeds[g]
        lam = [
            [[jnp.where(lasts == STEPS, seed[z][px][py], 0.0) for py in range(2)] for px in range(2)] for z in range(2)
        ]
        sums = [[zeros] * 5 for _ in range(2)]
        for t in range(STEPS - 1, 0, -1):
            state = plume[t]
            new = [[[None, None], [None, None]], [[None, None], [None, None]]]
            for z in range(2):
                k = ks[z]
                for px in range(2):
                    for py in range(2):
                        c, l = state[z][px][py], lam[z][px][py]
                        c_x, c_y = state[z][1 - px][py], state[z][px][1 - py]
                        l_x, l_y = lam[z][1 - px][py], lam[z][px][1 - py]
                        if px == 0:
                            to_east, to_west = c_x - c, c - pltpu.roll(c_x, 1, 0)
                            along_x = k["west"] * l_x + pltpu.roll(k["east"] * l_x, 1, 0)
                        else:
                            to_east, to_west = pltpu.roll(c_x, 7, 0) - c, c - c_x
                            along_x = pltpu.roll(k["west"] * l_x, 7, 0) + k["east"] * l_x
                        if py == 0:
                            to_north, to_south = c_y - c, c - pltpu.roll(c_y, 1, 1)
                            along_y = k["south"] * l_y + pltpu.roll(k["north"] * l_y, 1, 1)
                        else:
                            to_north, to_south = pltpu.roll(c_y, LANES - 1, 1) - c, c - c_y
                            along_y = pltpu.roll(k["south"] * l_y, LANES - 1, 1) + k["north"] * l_y
                        rise = state[1 - z][px][py] - 2.0 * c
                        for q, d in enumerate((to_east, to_west, to_north, to_south, rise)):
                            sums[z][q] = sums[z][q] + l * d
                        value = (k["centre"] * l + along_x) + (along_y + ks[1 - z]["diff"] * lam[1 - z][px][py])
                        new[z][px][py] = value + jnp.where(lasts == t, seed[z][px][py], 0.0)
            lam = new
        made = []
        for z in range(2):
            k = ks[z]
            made.append(chain(sums[z], k["diff"], k["wx"], k["wy"], k["fx"], k["fy"]))
        made = [[jnp.where(valid, made[z][f], 0.0) for z in range(2)] for f in range(3)]
        for r in members:
            here = slot == r % SLOTS
            x0, y0 = scalars[r, NSENS + 3], scalars[r, NSENS + 4]
            shift = (y0 - 8 * (r % SLOTS)) & (LANES - 1)
            for f in range(3):
                for z in range(2):
                    at = pl.ds((f * 2 + z) * ROWS + 8 + x0, 8)
                    grad[at, :] = grad[at, :] + pltpu.roll(jnp.where(here, made[f][z], 0.0), shift, 1)

    power = zeros
    for i in range(6 * ROWS // 8):
        g = grad[pl.ds(8 + i * 8, 8), :]
        power = power + g * g
    mean = jnp.sum(power, keepdims=True) * (1.0 / (6 * ROWS * LANES))
    scale = 1.0 / jnp.sqrt(mean + 1e-06)
    mine = me * rows + 8
    if rows % 8 == 0:
        mine = pl.multiple_of(mine, 8)
    direction_ref[...] = grad[pl.ds(mine, rows), :] * scale


def rounds(size):
    bits = [1 << i for i in range(size.bit_length() - 1)]
    return bits[2:] + bits[1::-1]


def solution(mesh):
    size = mesh.shape["rel"]
    bits = rounds(size)
    order = [0]
    for bit in bits:
        order = order + [at ^ bit for at in order]

    def local(coarse, background, sources, durations, counts, sensors, observed):
        rows = coarse.shape[0] // LANES
        block = -(-(rows + 2) // 8) * 8
        vmem = pl.BlockSpec(memory_space=pltpu.VMEM)
        smem = pl.BlockSpec(memory_space=pltpu.SMEM)
        packed = pl.pallas_call(
            pack_kernel,
            out_shape=jax.ShapeDtypeStruct((block, LANES), F32),
            in_specs=[vmem, vmem, vmem, smem, smem, smem],
            out_specs=vmem,
        )(coarse.reshape(rows, LANES), sensors, observed, sources, durations, counts)
        planes = pl.pallas_call(
            planes_kernel,
            out_shape=jax.ShapeDtypeStruct((FIELD, LANES), F32),
            in_specs=[vmem],
            out_specs=vmem,
            scratch_shapes=[pltpu.VMEM((4,) + background.shape[1:2] + (LANES,), F32)],
            compiler_params=pltpu.CompilerParams(vmem_limit_bytes=VMEM_LIMIT),
        )(background)
        held = packed
        for bit in bits:
            got = lax.ppermute(held, "rel", [(i, i ^ bit) for i in range(size)])
            if bit != bits[-1]:
                held = jnp.concatenate([held, got])
        direction, misfit = pl.pallas_call(
            functools.partial(gradient_kernel, order, rows),
            out_shape=(jax.ShapeDtypeStruct((rows, LANES), F32), jax.ShapeDtypeStruct((1,), F32)),
            in_specs=[vmem, vmem, vmem],
            out_specs=(vmem, smem),
            scratch_shapes=[
                pltpu.VMEM((6 * ROWS + 16, LANES), F32),
                pltpu.VMEM((14 * 2 * PLANE, LANES), F32),
                pltpu.VMEM((STEPS * FIELD, LANES), F32),
                pltpu.VMEM((FIELD, LANES), F32),
                pltpu.VMEM((FIELD, LANES), F32),
                pltpu.VMEM((10 * ROWS, LANES), F32),
                pltpu.VMEM((6 * ROWS + 16, LANES), F32),
                pltpu.VMEM((size, LANES), F32),
                pltpu.VMEM((size, LANES), F32),
                pltpu.VMEM((size, LANES), I32),
                pltpu.VMEM((size * NSENS, LANES), F32),
                pltpu.VMEM((size * NSENS, LANES), F32),
                pltpu.SMEM((size, LANES), I32),
                pltpu.SemaphoreType.DMA,
            ],
            compiler_params=pltpu.CompilerParams(vmem_limit_bytes=VMEM_LIMIT),
        )(held, got, planes)
        return direction.reshape(-1), misfit

    in_specs = (
        P(("grp", "rel")),
        P("grp", None, None),
        P(("grp", "rel")),
        P(("grp", "rel")),
        P(("grp", "rel")),
        P(("grp", "rel"), None),
        P(("grp", "rel"), None),
    )
    out_specs = (P(("grp", "rel")), P(("grp", "rel")))
    return jax.shard_map(local, mesh=mesh, in_specs=in_specs, out_specs=out_specs, check_vma=False)
```

time: 271 us -> 42.7 us (0.16)
  local copies, waits for them, and re-layouts: 79.9 us -> 0.01 us
  waiting for transfers between devices: 87 us -> 7.96 us
  other arithmetic: 58.6 us -> 2.27 us
  blocking collectives: 24.4 us -> 0 us
  Pallas kernels: 0 us -> 21.4 us
  between operations: 19.1 us -> 2.66 us
  starting transfers between devices: 0.04 us -> 7.98 us
    psum x1 -> x0, waiting for transfers between devices: 86.9 us -> none  [local(): gradient = lax.psum(local_grad, 'rel')]
    all_gather x1 -> x0, blocking collectives: 24.4 us -> none  [local(): whole = lax.all_gather(coarse, 'rel', axis=0, tiled=True)]
    pallas_call x0 -> x3, Pallas kernels: none -> 21.4 us  [the longest x1 19.3 us: local(): pl.pallas_call(functools.partial(gradient_kernel, order, rows), out_shape...]
    broadcast_in_dim x22 -> x0, local copies, waits for them, and re-layouts: 18.5 us -> none  [prolong(): fine = jnp.repeat(jnp.repeat(fields, 2, axis=2), 2, axis=3)]
    select_n x13 -> x0, other arithmetic: 18 us -> none  [the longest x7 9.15 us: advance(): return jnp.where(live, candidate, concentration)]
    select_n x10 -> x0, local copies, waits for them, and re-layouts: 16.5 us -> none  [the longest x2 3.98 us: advance(): return jnp.where(live, candidate, concentration)]
    gt x8 -> x0, local copies, waits for them, and re-layouts: 13.6 us -> none  [the longest x2 3.41 us: advance(): jnp.maximum(wind_y, 0.0) * (concentration - cell_south)]
    broadcast_in_dim x3 -> x0, other arithmetic: 11.3 us -> none  [the longest x1 7.02 us: prolong(): wind_y = 0.08 * jnp.tanh(fine[2])]
  transfers between devices with their start and end apart: 1 -> 4, of which waited for: 1 -> 4; matrix products, arithmetic and copies ran while one was open for 0% -> 0% of each run, Pallas kernels for 0% -> 2%
where the time goes in v1:
time: 42.7 us; the launch traced here: 42.3 us
  Pallas kernels  21.4 us (50%)
  starting transfers between devices  7.98 us (19%)
  waiting for transfers between devices  7.96 us (19%)
  between operations  2.66 us (6%)
  other arithmetic  2.27 us (5%)
    pallas_call x1, Pallas kernels, local(): pl.pallas_call(functools.partial(gradient_kernel, order, rows), out_shape...  19.3 us
    ppermute x4, starting transfers between devices, local(): got = lax.ppermute(held, 'rel', [(i, i ^ bit) for i in range(size)])  7.98 us
    ppermute x4, waiting for transfers between devices, local(): got = lax.ppermute(held, 'rel', [(i, i ^ bit) for i in range(size)])  7.96 us
    concatenate x3, other arithmetic, local(): held = jnp.concatenate([held, got])  2.27 us
    pallas_call x1, Pallas kernels, local(): pl.pallas_call(pack_kernel, out_shape=jax.ShapeDtypeStruct((block, LANES)...  1.43 us
  transfers between devices with their start and end apart: 4, of which 4 were waited for; matrix products, arithmetic and copies ran while one was open for 0% of the time, Pallas kernels for 2%

profile of v1, /device:TPU:0, one launch (start us, length us, event | category | flops | bytes accessed | tf_op | source)
XLA Modules:
  0.0 42.3 jit_solution(7974036423383126415)
XLA Ops:
  0.6 0.0 copy-start
  2.6 1.4 %shard_map.86 = f32[56,128]{1,0:T(8,128)} custom-call(f32[48,128]{1,0:T(8,128)} %bitcast.2, s32[1,64]{1,0:T(1,128)} %sensors_ref.1, f32[1,64]{1,0:T(1,128)} %observed_ref.1, s32[1]{0:T(128)S(6)} %copy.9.source_ref, s32[1]{0:T(128)S(6)} %copy.10.duration_ref, s32[1]{0:T(128)S(6)} %copy.11.count_ref), custom_call_target="tpu_custom_call" | custom-call | tf_op jit(solution)/shard_map/pallas_call | solution.py:517
  4.1 3.0 %collective-permute-start = (f32[56,128]{1,0:T(8,128)}, f32[56,128]{1,0:T(8,128)S(1)}, u32[]{:S(2)}, u32[]{:S(2)}) collective-permute-start(f32[56,128]{1,0:T(8,128)} %shard_map.86), channel_id=1, source_target_pairs={{0,4},{1,5},{2,6},{3,7},{4,0},{5,1},{6,2},{7,3},{8,12},{9,13},{10,... | collective-permute-start | bytes 86024 | tf_op jit(solution)/shard_map/ppermute | solution.py:533
  7.1 2.1 %collective-permute-done = f32[56,128]{1,0:T(8,128)S(1)} collective-permute-done((f32[56,128]{1,0:T(8,128)}, f32[56,128]{1,0:T(8,128)S(1)}, u32[]{:S(2)}, u32[]{:S(2)}) %collective-permute-start) | collective-permute-done | bytes 28704 | tf_op jit(solution)/shard_map/ppermute | solution.py:533
  9.1 0.8 %pad_maximum_fusion.2 = f32[112,128]{1,0:T(8,128)S(1)} fusion(f32[56,128]{1,0:T(8,128)S(1)} %collective-permute-done, f32[56,128]{1,0:T(8,128)} %shard_map.86), kind=kLoop, calls=%fused_computation.2 | loop fusion | flops 14336 | bytes 114688 | tf_op jit(solution)/shard_map/concatenate | solution.py:535
  9.9 3.0 %collective-permute-start.1 = (f32[112,128]{1,0:T(8,128)S(1)}, f32[112,128]{1,0:T(8,128)S(1)}, u32[]{:S(2)}, u32[]{:S(2)}) collective-permute-start(f32[112,128]{1,0:T(8,128)S(1)} %pad_maximum_fusion.2), channel_id=1, source_target_pairs={{0,8},{1,9},{2,10},{3,11},{4,12},{5,13},{6,14},{7,15},{8,0},{9,1},... | collective-permute-start | bytes 172040 | tf_op jit(solution)/shard_map/ppermute | solution.py:533
  12.9 2.2 %collective-permute-done.1 = f32[112,128]{1,0:T(8,128)S(1)} collective-permute-done((f32[112,128]{1,0:T(8,128)S(1)}, f32[112,128]{1,0:T(8,128)S(1)}, u32[]{:S(2)}, u32[]{:S(2)}) %collective-permute-start.1) | collective-permute-done | bytes 57376 | tf_op jit(solution)/shard_map/ppermute | solution.py:533
  15.1 0.8 %pad_maximum_fusion.1 = f32[224,128]{1,0:T(8,128)S(1)} fusion(f32[112,128]{1,0:T(8,128)S(1)} %collective-permute-done.1, f32[56,128]{1,0:T(8,128)S(1)} %collective-permute-done, f32[56,128]{1,0:T(8,128)} %shard_map.86), kind=kLoop, calls=%fused_computation.1 | loop fusion | flops 57344 | bytes 229376 | tf_op jit(solution)/shard_map/concatenate | solution.py:535
  15.8 1.9 %collective-permute-start.2 = (f32[224,128]{1,0:T(8,128)S(1)}, f32[224,128]{1,0:T(8,128)S(1)}, u32[]{:S(2)}, u32[]{:S(2)}) collective-permute-start(f32[224,128]{1,0:T(8,128)S(1)} %pad_maximum_fusion.1), channel_id=1, source_target_pairs={{0,2},{1,3},{2,0},{3,1},{4,6},{5,7},{6,4},{7,5},{8,10},{9,11},{10,... | collective-permute-start | bytes 344072 | tf_op jit(solution)/shard_map/ppermute | solution.py:533
  17.7 2.9 %collective-permute-done.2 = f32[224,128]{1,0:T(8,128)S(1)} collective-permute-done((f32[224,128]{1,0:T(8,128)S(1)}, f32[224,128]{1,0:T(8,128)S(1)}, u32[]{:S(2)}, u32[]{:S(2)}) %collective-permute-start.2) | collective-permute-done | bytes 114720 | tf_op jit(solution)/shard_map/ppermute | solution.py:533
  20.6 0.8 %pad_maximum_fusion.first_ref = f32[448,128]{1,0:T(8,128)S(1)} fusion(f32[224,128]{1,0:T(8,128)S(1)} %collective-permute-done.2, f32[112,128]{1,0:T(8,128)S(1)} %collective-permute-done.1, f32[56,128]{1,0:T(8,128)S(1)} %collective-permute-done, f32[56,128]{1,0:T(8,128)} %shard_map.86), kind=kLoop, calls=%fused_computation | loop fusion | flops 172032 | bytes 458752 | tf_op jit(solution)/shard_map/concatenate | solution.py:535
  21.4 0.1 collective-permute-start.3
  21.5 0.0 copy-done
  21.5 0.7 %shard_map.87.planes_ref = f32[1152,128]{1,0:T(8,128)S(1)} custom-call(f32[2,256,256]{2,1,0:T(8,128)S(1)} %copy-done), custom_call_target="tpu_custom_call" | custom-call | tf_op jit(solution)/shard_map/pallas_call | solution.py:523
  22.2 0.8 %collective-permute-done.3.second_ref = f32[448,128]{1,0:T(8,128)S(1)} collective-permute-done((f32[448,128]{1,0:T(8,128)S(1)}, f32[448,128]{1,0:T(8,128)S(1)}, u32[]{:S(2)}, u32[]{:S(2)}) %collective-permute-start.3) | collective-permute-done | bytes 229408 | tf_op jit(solution)/shard_map/ppermute | solution.py:533
  23.0 19.3 %shard_map.88 = (f32[48,128]{1,0:T(8,128)}, f32[1]{0:T(128)}) custom-call(f32[448,128]{1,0:T(8,128)S(1)} %pad_maximum_fusion.first_ref, f32[448,128]{1,0:T(8,128)S(1)} %collective-permute-done.3.second_ref, f32[1152,128]{1,0:T(8,128)S(1)} %shard_map.87.planes_ref), custom_call_target="tpu_custom_call" | custom-call | tf_op jit(solution)/shard_map/pallas_call | solution.py:536
Async XLA Ops:
  0.6 20.9 %copy-start = (f32[2,256,256]{2,1,0:T(8,128)S(1)}, f32[2,256,256]{2,1,0:T(8,128)}, u32[]{:S(2)}) copy-start(f32[2,256,256]{2,1,0:T(8,128)} %background_ref.1) | copy-start | bytes 1572868
  4.1 5.1 %collective-permute-start = (f32[56,128]{1,0:T(8,128)}, f32[56,128]{1,0:T(8,128)S(1)}, u32[]{:S(2)}, u32[]{:S(2)}) collective-permute-start(f32[56,128]{1,0:T(8,128)} %shard_map.86), channel_id=1, source_target_pairs={{0,4},{1,5},{2,6},{3,7},{4,0},{5,1},{6,2},{7,3},{8,12},{9,13},{10,... | collective-permute-start | bytes 86024 | tf_op jit(solution)/shard_map/ppermute | solution.py:533
  9.9 5.2 %collective-permute-start.1 = (f32[112,128]{1,0:T(8,128)S(1)}, f32[112,128]{1,0:T(8,128)S(1)}, u32[]{:S(2)}, u32[]{:S(2)}) collective-permute-start(f32[112,128]{1,0:T(8,128)S(1)} %pad_maximum_fusion.2), channel_id=1, source_target_pairs={{0,8},{1,9},{2,10},{3,11},{4,12},{5,13},{6,14},{7,15},{8,0},{9,1},... | collective-permute-start | bytes 172040 | tf_op jit(solution)/shard_map/ppermute | solution.py:533
  15.8 4.8 %collective-permute-start.2 = (f32[224,128]{1,0:T(8,128)S(1)}, f32[224,128]{1,0:T(8,128)S(1)}, u32[]{:S(2)}, u32[]{:S(2)}) collective-permute-start(f32[224,128]{1,0:T(8,128)S(1)} %pad_maximum_fusion.1), channel_id=1, source_target_pairs={{0,2},{1,3},{2,0},{3,1},{4,6},{5,7},{6,4},{7,5},{8,10},{9,11},{10,... | collective-permute-start | bytes 344072 | tf_op jit(solution)/shard_map/ppermute | solution.py:533
  21.4 1.6 %collective-permute-start.3 = (f32[448,128]{1,0:T(8,128)S(1)}, f32[448,128]{1,0:T(8,128)S(1)}, u32[]{:S(2)}, u32[]{:S(2)}) collective-permute-start(f32[448,128]{1,0:T(8,128)S(1)} %pad_maximum_fusion.first_ref), channel_id=1, source_target_pairs={{0,1},{1,0},{2,3},{3,2},{4,5},{5,4},{6,7},{7,6},{8,9},{9,8},{10,11... | collective-permute-start | bytes 688136 | tf_op jit(solution)/shard_map/ppermute | solution.py:533

commit v2 on v1

--- a/solution.py
+++ b/solution.py
@@ -20,7 +20,7 @@
 F32, BF16, I32 = jnp.float32, jnp.bfloat16, jnp.int32
 
 
-def loop(first, end, unroll=1):
+def loop(first, end, unroll=None):
     def run(body):
         lax.fori_loop(first, end, body, None, unroll=unroll)
 
@@ -36,15 +36,23 @@
     return high, (value - high.astype(F32)).astype(BF16)
 
 
-def pack_kernel(coarse_ref, sensors_ref, observed_ref, source_ref, duration_ref, count_ref, out_ref):
+def pack_kernel(source_ref, duration_ref, count_ref, coarse_ref, sensors_ref, observed_ref, out_ref, *rest):
+    sensors, observed, sems = rest
     rows = coarse_ref.shape[0]
-    out_ref[...] = jnp.zeros_like(out_ref)
-    out_ref[pl.ds(0, rows), :] = coarse_ref[...]
-    out_ref[pl.ds(rows, 1), pl.ds(0, NSENS)] = sensors_ref[...].astype(F32)
-    out_ref[pl.ds(rows, 1), pl.ds(NSENS, NSENS)] = observed_ref[...]
+    pairs = ((coarse_ref, out_ref.at[pl.ds(0, rows), :]), (sensors_ref, sensors), (observed_ref, observed))
+    copies = [pltpu.make_async_copy(src, dst, sems.at[i]) for i, (src, dst) in enumerate(pairs)]
+    for copy in copies:
+        copy.start()
     lane = lax.broadcasted_iota(I32, (1, LANES), 1)
     record = jnp.where(lane == 0, source_ref[0], jnp.where(lane == 1, duration_ref[0], count_ref[0]))
+    record = jnp.where(lane == 3, lax.axis_index("rel"), record)
+    for copy in copies:
+        copy.wait()
+    out_ref[pl.ds(rows, 1), pl.ds(0, NSENS)] = sensors[...].astype(F32)
+    out_ref[pl.ds(rows, 1), pl.ds(NSENS, NSENS)] = observed[...]
     out_ref[pl.ds(rows + 1, 1), :] = record.astype(F32)
+    spare = out_ref.shape[0] - rows - 2
+    out_ref[pl.ds(rows + 2, spare), :] = jnp.zeros((spare, LANES), F32)
 
 
 def planes_kernel(background_ref, out_ref, half_ref):
@@ -108,29 +116,61 @@
         sens_rows[pl.ds(owner, 1), :] = ref[pl.ds(at + rows, 1), :]
         meta_rows[pl.ds(owner, 1), :] = ref[pl.ds(at + rows + 1, 1), :]
 
+    half = blocks // 2
     wide = lax.broadcasted_iota(I32, (blocks, LANES), 1)
-    release = lax.broadcasted_iota(I32, (blocks, LANES), 0)
-    sens = jnp.where(wide < NSENS, sens_rows[...], 0.0).astype(I32)
-    meta = meta_rows[...].astype(I32)
-    source = jnp.broadcast_to(meta[:, 0:1], (blocks, LANES))
-    duration = jnp.broadcast_to(meta[:, 1:2], (blocks, LANES))
-    count = jnp.broadcast_to(meta[:, 2:3], (blocks, LANES))
+    place = lax.broadcasted_iota(I32, (blocks, LANES), 0)
+    counts = jnp.broadcast_to(meta_rows[:, 2:3], (blocks, LANES))
+    across = jnp.broadcast_to(counts.T[0:1, :], (blocks, blocks))
+    down, left, top = counts[:, :blocks], wide[:, :blocks], place[:, :blocks]
+    ahead = (down > across) | ((down == across) & (top < left))
+    rank = jnp.sum(ahead.astype(F32), axis=0, keepdims=True)
+    wanted = jnp.where(top < half, 2 * top, 2 * (top - half) + 1).astype(F32)
+    order_by = (jnp.broadcast_to(rank, (blocks, blocks)) == wanted).astype(F32)
+    at_least = jnp.sum((counts >= (wide - 8).astype(F32)).astype(F32), axis=0, keepdims=True)
+    sorted_rows = jnp.dot(
+        order_by,
+        jnp.concatenate([sens_rows[...], meta_rows[...]], axis=1),
+        precision=lax.Precision.HIGHEST,
+        preferred_element_type=F32,
+    )
+    sorted_sens, meta = sorted_rows[:, :LANES], jnp.round(sorted_rows[:, LANES:]).astype(I32)
+
+    pair_lane, pair_row = wide[:half], place[:half]
+    first = pair_lane < NSENS
+
+    def paired(value):
+        return jnp.where(first, value[:half], value[half:])
+
+    def spread(value):
+        return jnp.broadcast_to(value, (blocks, LANES))
+
+    turned = pltpu.roll(sorted_sens, NSENS, 1)
+    sens = jnp.round(jnp.where(first, sorted_sens[:half], turned[half:])).astype(I32)
+    watched = jnp.where(first, turned[:half], sorted_sens[half:])
+    source, count, owner_of = spread(meta[:, 0:1]), spread(meta[:, 2:3]), spread(meta[:, 3:4])
+    left_x = (((source >> 8) & 255) >> 1) - 3
+    left_y = ((source & 255) >> 1) - 3
     fine_x, fine_y = (sens >> 8) & 255, sens & 255
     plane = (sens >> 16) * 4 + (fine_x & 1) * 2 + (fine_y & 1)
     cell_x, cell_y = fine_x >> 1, fine_y >> 1
-    left_x = (((source >> 8) & 255) >> 1) - 3
-    left_y = ((source & 255) >> 1) - 3
-    off_x, off_y = cell_x - left_x, cell_y - left_y
+    off_x, off_y = cell_x - paired(left_x), cell_y - paired(left_y)
     inside = (off_x >= 0) & (off_x < 8) & (off_y >= 0) & (off_y < 8)
+    slot_of = (2 * pair_row + jnp.where(first, 0, 1)) % SLOTS
     patch_row = jnp.where(inside, plane * 8 + off_x, -1)
-    patch_lane = jnp.where(inside, (release % SLOTS) * 8 + off_y, -1)
-    address = (count - 1) * FIELD + plane * PLANE + PAD + cell_x
-    row_id = (plane * ROWS + cell_x).astype(F32)
-    for at, value in ((0, source), (1, duration), (2, count), (3, left_x), (4, left_y)):
-        address = jnp.where(wide == NSENS + at, value, address)
-    table[...] = address
+    patch_lane = jnp.where(inside, slot_of * 8 + off_y, -1)
+    address = plane * PLANE + PAD + cell_x
+    mine_of = paired(owner_of) == me
+    for at, value in ((4, left_x), (5, left_y), (6, spread(meta[:, 0:1]))):
+        meta = jnp.where(wide == at, value, meta)
+    meta = jnp.where(wide >= 8, jnp.broadcast_to(at_least, (blocks, LANES)).astype(I32), meta)
+    table[pl.ds(0, half), :] = address + (paired(count) - 1) * FIELD
+    table[pl.ds(half, half), :] = address
+    table[pl.ds(blocks, blocks), :] = meta
     copy = pltpu.make_async_copy(table, scalars, sem)
     copy.start()
+
+    def about(j, lane_at):
+        return scalars[blocks + (j % 2) * half + j // 2, lane_at]
 
     names = ("centre", "east", "west", "north", "south", "diff", "south0", "north1", "northr", "southl", "wx", "wy", "fx", "fy")
     index = {name: i for i, name in enumerate(names)}
@@ -185,7 +225,7 @@
         return own, odd, even
 
     def forward(src, src_base, dst, dst_base):
-        @loop(0, ROWS // 8, unroll=2)
+        @loop(0, ROWS // 8, unroll=16)
         def _(i, carry):
             x = pl.multiple_of(i * 8, 8)
             own, odd, even = load(src, src_base, x)
@@ -217,11 +257,11 @@
 
     copy.wait()
 
-    @loop(0, blocks)
-    def _(r, carry):
-        to = pl.multiple_of(r * NSENS, NSENS)
-        for s in range(NSENS):
-            gathered[pl.ds(to + s, 1), :] = hist[pl.ds(scalars[r, s], 1), :]
+    @loop(0, half)
+    def _(j, carry):
+        to = pl.multiple_of(j * LANES, LANES)
+        for s in range(LANES):
+            gathered[pl.ds(to + s, 1), :] = hist[pl.ds(scalars[j, s], 1), :]
         return carry
 
     slot = lane >> 3
@@ -232,8 +272,7 @@
         at_x, at_y, of_plane, lasts, emits = (jnp.zeros((8, LANES), I32) for _ in range(5))
         for r in members:
             here = slot == r % SLOTS
-            src, dur, cnt = scalars[r, NSENS], scalars[r, NSENS + 1], scalars[r, NSENS + 2]
-            x0, y0 = scalars[r, NSENS + 3], scalars[r, NSENS + 4]
+            src, dur, cnt, x0, y0 = (about(r, at) for at in (0, 1, 2, 4, 5))
             shift = (8 * (r % SLOTS) - y0) & (LANES - 1)
             for f in range(3):
                 for z in range(2):
@@ -278,80 +317,64 @@
             state = new
         patches.append((ks, valid, lasts, plume, state))
 
-    lane_f, row_f = patch_lane.astype(F32), patch_row.astype(F32)
-    first_half = wide < NSENS
-    turn_a = jnp.where(first_half, cell_y.astype(F32), pltpu.roll(lane_f, NSENS, 1)).T
-    turn_b = jnp.where(first_half, row_f, pltpu.roll(row_id, NSENS, 1)).T
-    turn_c = sens_rows[...].T
-    lane64 = lax.broadcasted_iota(I32, (NSENS, LANES), 1).astype(F32)
-    lane_sq = lax.broadcasted_iota(I32, (NSENS, NSENS), 1).astype(F32)
-    sub_sq = lax.broadcasted_iota(I32, (NSENS, NSENS), 0).astype(F32)
-    batch = (lane_sq.astype(I32) // BATCH) == (sub_sq.astype(I32) // BATCH)
-    loss = jnp.zeros((NSENS, LANES), F32)
+    def row_of(value, j):
+        return jnp.broadcast_to(value[j : j + 1, :], (LANES, LANES))
+
+    def with_rows(a, b):
+        return lax.dot_general(a, b, (((1,), (1,)), ((), ())), preferred_element_type=F32)
+
+    sub_sq = lax.broadcasted_iota(I32, (LANES, LANES), 0)
+    lane_sq = lax.broadcasted_iota(I32, (LANES, LANES), 1)
+    diagonal = sub_sq == lane_sq
+    batch = (lane_sq // BATCH) == (sub_sq // BATCH)
+    row_id = address.astype(F32)
+    row_down = row_id.T
+    loss = jnp.zeros((1, LANES), F32)
     seeds = []
     for g in range(groups):
-        members = range(g * SLOTS, min(blocks, (g + 1) * SLOTS))
         final = patches[g][4]
         flat = jnp.concatenate([final[z][px][py] for z in range(2) for px in range(2) for py in range(2)], axis=0)
-        flat = jnp.concatenate(split(flat), axis=1)
-        seed = jnp.zeros((NSENS, 2 * LANES), F32)
-        for r in members:
-            def column(turned, half):
-                return jnp.broadcast_to(turned[half * NSENS : (half + 1) * NSENS, r : r + 1], (NSENS, LANES))
-
-            own_lane, own_patch = column(turn_a, 0), column(turn_a, 1)
-            own_row, own_cell = column(turn_b, 0), column(turn_b, 1)
-            watched = column(turn_c, 1)
-            pick = (own_row[:, :NSENS] == lane_sq).astype(BF16)
-            near = jnp.dot(pick, flat, preferred_element_type=F32)
-            near = near[:, :LANES] + near[:, LANES:]
-            on_lane, on_patch = lane64 == own_lane, lane64 == own_patch
-            value = jnp.where(on_lane, gathered[pl.ds(r * NSENS, NSENS), :], 0.0)
-            value = value + jnp.where(on_patch, near, 0.0)
-            residual = jnp.sum(value, axis=1, keepdims=True) - watched
-            loss = jnp.where(me == r, residual * residual, loss)
-            same = own_cell[:, :NSENS] == jnp.broadcast_to(row_id[r : r + 1, :NSENS], (NSENS, NSENS))
-            same = (same & batch).astype(BF16)
-            spread = jnp.dot(
-                same,
-                jnp.concatenate(split(jnp.where(on_lane, residual, 0.0)), axis=1),
-                preferred_element_type=F32,
-            )
-            scattered[pl.ds(r * NSENS, NSENS), :] = spread[:, :LANES] + spread[:, LANES:]
-            put = (sub_sq == jnp.broadcast_to(row_f[r : r + 1, :NSENS], (NSENS, NSENS))).astype(BF16)
-            seed = seed + jnp.dot(
-                put,
-                jnp.concatenate(split(jnp.where(on_patch, residual, 0.0)), axis=1),
-                preferred_element_type=F32,
-            )
-        seed = seed[:, :LANES] + seed[:, LANES:]
+        flat = jnp.concatenate(split(flat), axis=0)
+        seed = jnp.zeros((LANES, LANES), F32)
+        for j in range(g * SLOTS // 2, min(half, (g + 1) * SLOTS // 2)):
+            at_lane = (sub_sq == row_of(cell_y, j)).astype(F32).astype(BF16)
+            at_patch = (sub_sq == row_of(patch_lane, j)).astype(F32).astype(BF16)
+            put = sub_sq[:NSENS] == row_of(patch_row, j)[:NSENS]
+            high, low = split(gathered[pl.ds(j * LANES, LANES), :])
+            far = jnp.dot(high, at_lane, preferred_element_type=F32) + jnp.dot(low, at_lane, preferred_element_type=F32)
+            far = jnp.sum(jnp.where(diagonal, far, 0.0), axis=0, keepdims=True)
+            near = jnp.dot(flat, at_patch, preferred_element_type=F32)
+            near = jnp.sum(jnp.where(put, near[:NSENS] + near[NSENS:], 0.0), axis=0, keepdims=True)
+            residual = far + near - watched[j : j + 1, :]
+            loss = loss + jnp.where(mine_of[j : j + 1, :], residual * residual, 0.0)
+            same = (jnp.broadcast_to(row_down[:, j : j + 1], (LANES, LANES)) == row_of(row_id, j)) & batch
+            high, low = split(jnp.where(same, jnp.broadcast_to(residual, (LANES, LANES)), 0.0))
+            scattered[pl.ds(j * LANES, LANES), :] = with_rows(high, at_lane) + with_rows(low, at_lane)
+            put = jnp.where(put, jnp.broadcast_to(residual, (NSENS, LANES)), 0.0)
+            seed = seed + with_rows(jnp.concatenate(split(put), axis=0), at_patch)
+        seed = seed[:NSENS] + seed[NSENS:]
         seeds.append(
             [[[seed[((z * 2 + px) * 2 + py) * 8 :][:8] for py in range(2)] for px in range(2)] for z in range(2)]
         )
-    misfit_ref[0] = jnp.sum(loss[:, 0:1]) * (0.5 / NSENS)
+    misfit_ref[0] = jnp.sum(loss) * (0.5 / NSENS)
 
     def seed_sensors(ref, t):
-        @loop(0, blocks)
-        def _(r, carry):
-            @pl.when(scalars[r, NSENS + 2] == t)
-            def _():
-                at = pl.multiple_of(r * NSENS, NSENS)
-                for part in range(0, NSENS, BATCH):
-                    spots, news = [], []
-                    for s in range(part, part + BATCH):
-                        spot = pl.ds(scalars[r, s] - (t - 1) * FIELD, 1)
-                        spots.append(spot)
-                        news.append(ref[spot, :] + scattered[pl.ds(at + s, 1), :])
-                    for spot, new in zip(spots, news):
-                        ref[spot, :] = new
-
+        @loop(scalars[blocks, 8 + t + 1], scalars[blocks, 8 + t])
+        def _(j, carry):
+            row, column = j // 2, (j % 2) * NSENS
+            at = pl.multiple_of(j * NSENS, NSENS)
+            for part in range(0, NSENS, BATCH):
+                spots = [pl.ds(scalars[half + row, column + s], 1) for s in range(part, part + BATCH)]
+                news = [ref[spot, :] + scattered[pl.ds(at + part + s, 1), :] for s, spot in enumerate(spots)]
+                for spot, new in zip(spots, news):
+                    ref[spot, :] = new
             return carry
 
     def acc_at(q, z, x):
         return pl.ds((q * 2 + z) * ROWS + x, 8)
 
     def backward(src, dst, conc, conc_base, first, last):
-        @loop(0, ROWS // 8, unroll=2)
+        @loop(0, ROWS // 8, unroll=16)
         def _(i, carry):
             x = pl.multiple_of(i * 8, 8)
             lam, lam_odd, lam_even = load(src, 0, x)
@@ -425,7 +448,7 @@
         g0 = (to_east - to_west + to_north - to_south + rise) * diff
         return g0, wind(wx, to_west, to_east, fx), wind(wy, to_south, to_north, fy)
 
-    @loop(0, ROWS // 8, unroll=2)
+    @loop(0, ROWS // 8, unroll=16)
     def _(i, carry):
         x = pl.multiple_of(i * 8, 8)
         for z in range(2):
@@ -478,12 +501,16 @@
         made = [[jnp.where(valid, made[z][f], 0.0) for z in range(2)] for f in range(3)]
         for r in members:
             here = slot == r % SLOTS
-            x0, y0 = scalars[r, NSENS + 3], scalars[r, NSENS + 4]
+            x0, y0 = about(r, 4), about(r, 5)
             shift = (y0 - 8 * (r % SLOTS)) & (LANES - 1)
-            for f in range(3):
-                for z in range(2):
-                    at = pl.ds((f * 2 + z) * ROWS + 8 + x0, 8)
-                    grad[at, :] = grad[at, :] + pltpu.roll(jnp.where(here, made[f][z], 0.0), shift, 1)
+            spots = [pl.ds((f * 2 + z) * ROWS + 8 + x0, 8) for f in range(3) for z in range(2)]
+            news = [
+                grad[spots[f * 2 + z], :] + pltpu.roll(jnp.where(here, made[f][z], 0.0), shift, 1)
+                for f in range(3)
+                for z in range(2)
+            ]
+            for spot, new in zip(spots, news):
+                grad[spot, :] = new
 
     power = zeros
     for i in range(6 * ROWS // 8):
@@ -516,10 +543,15 @@
         smem = pl.BlockSpec(memory_space=pltpu.SMEM)
         packed = pl.pallas_call(
             pack_kernel,
-            out_shape=jax.ShapeDtypeStruct((block, LANES), F32),
-            in_specs=[vmem, vmem, vmem, smem, smem, smem],
+            out_shape=pltpu.VMEM((block, LANES), F32),
+            in_specs=[smem] * 3 + [pl.BlockSpec(memory_space=pl.ANY)] * 3,
             out_specs=vmem,
-        )(coarse.reshape(rows, LANES), sensors, observed, sources, durations, counts)
+            scratch_shapes=[
+                pltpu.VMEM((1, NSENS), I32),
+                pltpu.VMEM((1, NSENS), F32),
+                pltpu.SemaphoreType.DMA((3,)),
+            ],
+        )(sources, durations, counts, coarse.reshape(rows, LANES), sensors, observed)
         planes = pl.pallas_call(
             planes_kernel,
             out_shape=jax.ShapeDtypeStruct((FIELD, LANES), F32),
@@ -528,11 +560,12 @@
             scratch_shapes=[pltpu.VMEM((4,) + background.shape[1:2] + (LANES,), F32)],
             compiler_params=pltpu.CompilerParams(vmem_limit_bytes=VMEM_LIMIT),
         )(background)
-        held = packed
+        held = packed.reshape(-1)
         for bit in bits:
             got = lax.ppermute(held, "rel", [(i, i ^ bit) for i in range(size)])
             if bit != bits[-1]:
-                held = jnp.concatenate([held, got])
+                own = lax.optimization_barrier(jnp.concatenate([held, jnp.zeros_like(held)]))
+                held = lax.optimization_barrier(lax.dynamic_update_slice(own, got, (held.shape[0],)))
         direction, misfit = pl.pallas_call(
             functools.partial(gradient_kernel, order, rows),
             out_shape=(jax.ShapeDtypeStruct((rows, LANES), F32), jax.ShapeDtypeStruct((1,), F32)),
@@ -548,14 +581,14 @@
                 pltpu.VMEM((6 * ROWS + 16, LANES), F32),
                 pltpu.VMEM((size, LANES), F32),
                 pltpu.VMEM((size, LANES), F32),
-                pltpu.VMEM((size, LANES), I32),
+                pltpu.VMEM((2 * size, LANES), I32),
                 pltpu.VMEM((size * NSENS, LANES), F32),
                 pltpu.VMEM((size * NSENS, LANES), F32),
-                pltpu.SMEM((size, LANES), I32),
+                pltpu.SMEM((2 * size, LANES), I32),
                 pltpu.SemaphoreType.DMA,
             ],
             compiler_params=pltpu.CompilerParams(vmem_limit_bytes=VMEM_LIMIT),
-        )(held, got, planes)
+        )(held.reshape(-1, LANES), got.reshape(-1, LANES), planes)
         return direction.reshape(-1), misfit
 
     in_specs = (

time: 42.7 us -> 32.5 us (0.76)
  Pallas kernels: 21.4 us -> 13.9 us
  other arithmetic: 2.27 us -> 0 us
    pallas_call x1, Pallas kernels: 19.3 us -> 12.3 us  [local(): pl.pallas_call(functools.partial(gradient_kernel, order, rows), out_shape...]
    concatenate x3 -> x0, other arithmetic: 2.27 us -> none  [local(): held = jnp.concatenate([held, got])]
    pallas_call x1, Pallas kernels: 1.43 us -> 0.89 us  [local(): pl.pallas_call(pack_kernel, out_shape=pltpu.VMEM((block, LANES), F32), in...]
where the time goes in v2:
time: 32.5 us; the launch traced here: 32.3 us
  Pallas kernels  13.9 us (43%)
  starting transfers between devices  8.04 us (25%)
  waiting for transfers between devices  7.71 us (24%)
  between operations  2.62 us (8%)
    pallas_call x1, Pallas kernels, local(): pl.pallas_call(functools.partial(gradient_kernel, order, rows), out_shape...  12.3 us
    ppermute x4, starting transfers between devices, local(): got = lax.ppermute(held, 'rel', [(i, i ^ bit) for i in range(size)])  8.04 us
    ppermute x4, waiting for transfers between devices, local(): got = lax.ppermute(held, 'rel', [(i, i ^ bit) for i in range(size)])  7.71 us
    pallas_call x1, Pallas kernels, local(): pl.pallas_call(pack_kernel, out_shape=pltpu.VMEM((block, LANES), F32), in...  0.89 us
    pallas_call x1, Pallas kernels, local(): pl.pallas_call(planes_kernel, out_shape=jax.ShapeDtypeStruct((FIELD, LANE...  0.65 us
  transfers between devices with their start and end apart: 4, of which 4 were waited for; matrix products, arithmetic and copies ran while one was open for 0% of the time, Pallas kernels for 2%

profile of v2, /device:TPU:0, one launch (start us, length us, event | category | flops | bytes accessed | tf_op | source)
XLA Modules:
  0.0 32.3 jit_solution(5443633211813729734)
XLA Ops:
  2.6 0.0 copy-start
  2.6 0.9 %shard_map.86 = f32[56,128]{1,0:T(8,128)S(1)} custom-call(s32[1]{0:T(128)S(6)} %copy.12.source_ref, s32[1]{0:T(128)S(6)} %copy.13.duration_ref, s32[1]{0:T(128)S(6)} %copy.14.count_ref, f32[48,128]{1,0:T(8,128)} %bitcast.9, s32[1,64]{1,0:T(1,128)} %sensors_ref.1, f32[1,64]{1,0:T(1,128)} %observed_ref.1), custom_call_target="tpu_custom_call" | custom-call | tf_op jit(solution)/shard_map/pallas_call | solution.py:544
  3.5 3.1 %collective-permute-start = (f32[7168]{0:T(1024)S(1)}, f32[7168]{0:T(1024)S(1)}, u32[]{:S(2)}, u32[]{:S(2)}) collective-permute-start(f32[7168]{0:T(1024)S(1)} %bitcast.7), channel_id=1, source_target_pairs={{0,4},{1,5},{2,6},{3,7},{4,0},{5,1},{6,2},{7,3},{8,12},{9,13},{10,... | collective-permute-start | bytes 86024 | tf_op jit(solution)/shard_map/ppermute | solution.py:565
  6.6 1.8 %collective-permute-done = f32[7168]{0:T(1024)S(1)} collective-permute-done((f32[7168]{0:T(1024)S(1)}, f32[7168]{0:T(1024)S(1)}, u32[]{:S(2)}, u32[]{:S(2)}) %collective-permute-start) | collective-permute-done | bytes 28704 | tf_op jit(solution)/shard_map/ppermute | solution.py:565
  8.4 3.0 %collective-permute-start.1 = (f32[14336]{0:T(1024)S(1)}, f32[14336]{0:T(1024)S(1)}, u32[]{:S(2)}, u32[]{:S(2)}) collective-permute-start(f32[14336]{0:T(1024)S(1)} %constant_dynamic-update-slice_fusion.2), channel_id=1, source_target_pairs={{0,8},{1,9},{2,10},{3,11},{4,12},{5,13},{6,14},{7,15},{8,0},{9,1},... | collective-permute-start | bytes 172040 | tf_op jit(solution)/shard_map/ppermute | solution.py:565
  11.5 2.1 %collective-permute-done.1 = f32[14336]{0:T(1024)S(1)} collective-permute-done((f32[14336]{0:T(1024)S(1)}, f32[14336]{0:T(1024)S(1)}, u32[]{:S(2)}, u32[]{:S(2)}) %collective-permute-start.1) | collective-permute-done | bytes 57376 | tf_op jit(solution)/shard_map/ppermute | solution.py:565
  13.6 1.9 %collective-permute-start.2 = (f32[28672]{0:T(1024)S(1)}, f32[28672]{0:T(1024)S(1)}, u32[]{:S(2)}, u32[]{:S(2)}) collective-permute-start(f32[28672]{0:T(1024)S(1)} %constant_dynamic-update-slice_fusion.1), channel_id=1, source_target_pairs={{0,2},{1,3},{2,0},{3,1},{4,6},{5,7},{6,4},{7,5},{8,10},{9,11},{10,... | collective-permute-start | bytes 344072 | tf_op jit(solution)/shard_map/ppermute | solution.py:565
  15.5 2.9 %collective-permute-done.2 = f32[28672]{0:T(1024)S(1)} collective-permute-done((f32[28672]{0:T(1024)S(1)}, f32[28672]{0:T(1024)S(1)}, u32[]{:S(2)}, u32[]{:S(2)}) %collective-permute-start.2) | collective-permute-done | bytes 114720 | tf_op jit(solution)/shard_map/ppermute | solution.py:565
  18.4 0.1 collective-permute-start.3
  18.5 0.0 copy-done
  18.5 0.7 %shard_map.87.planes_ref = f32[1152,128]{1,0:T(8,128)S(1)} custom-call(f32[2,256,256]{2,1,0:T(8,128)S(1)} %copy-done), custom_call_target="tpu_custom_call" | custom-call | tf_op jit(solution)/shard_map/pallas_call | solution.py:555
  19.2 0.8 %collective-permute-done.3 = f32[57344]{0:T(1024)S(1)} collective-permute-done((f32[57344]{0:T(1024)S(1)}, f32[57344]{0:T(1024)S(1)}, u32[]{:S(2)}, u32[]{:S(2)}) %collective-permute-start.3) | collective-permute-done | bytes 229408 | tf_op jit(solution)/shard_map/ppermute | solution.py:565
  20.0 12.3 %shard_map.88 = (f32[48,128]{1,0:T(8,128)}, f32[1]{0:T(128)}) custom-call(f32[448,128]{1,0:T(8,128)S(1)} %bitcast.5, f32[448,128]{1,0:T(8,128)S(1)} %bitcast.6, f32[1152,128]{1,0:T(8,128)S(1)} %shard_map.87.planes_ref), custom_call_target="tpu_custom_call" | custom-call | tf_op jit(solution)/shard_map/pallas_call | solution.py:569
  (6 shorter events, 0.0 us)
Async XLA Ops:
  2.6 15.9 %copy-start = (f32[2,256,256]{2,1,0:T(8,128)S(1)}, f32[2,256,256]{2,1,0:T(8,128)}, u32[]{:S(2)}) copy-start(f32[2,256,256]{2,1,0:T(8,128)} %background_ref.1) | copy-start | bytes 1572868
  3.5 4.9 %collective-permute-start = (f32[7168]{0:T(1024)S(1)}, f32[7168]{0:T(1024)S(1)}, u32[]{:S(2)}, u32[]{:S(2)}) collective-permute-start(f32[7168]{0:T(1024)S(1)} %bitcast.7), channel_id=1, source_target_pairs={{0,4},{1,5},{2,6},{3,7},{4,0},{5,1},{6,2},{7,3},{8,12},{9,13},{10,... | collective-permute-start | bytes 86024 | tf_op jit(solution)/shard_map/ppermute | solution.py:565
  8.4 5.2 %collective-permute-start.1 = (f32[14336]{0:T(1024)S(1)}, f32[14336]{0:T(1024)S(1)}, u32[]{:S(2)}, u32[]{:S(2)}) collective-permute-start(f32[14336]{0:T(1024)S(1)} %constant_dynamic-update-slice_fusion.2), channel_id=1, source_target_pairs={{0,8},{1,9},{2,10},{3,11},{4,12},{5,13},{6,14},{7,15},{8,0},{9,1},... | collective-permute-start | bytes 172040 | tf_op jit(solution)/shard_map/ppermute | solution.py:565
  13.6 4.8 %collective-permute-start.2 = (f32[28672]{0:T(1024)S(1)}, f32[28672]{0:T(1024)S(1)}, u32[]{:S(2)}, u32[]{:S(2)}) collective-permute-start(f32[28672]{0:T(1024)S(1)} %constant_dynamic-update-slice_fusion.1), channel_id=1, source_target_pairs={{0,2},{1,3},{2,0},{3,1},{4,6},{5,7},{6,4},{7,5},{8,10},{9,11},{10,... | collective-permute-start | bytes 344072 | tf_op jit(solution)/shard_map/ppermute | solution.py:565
  18.4 1.6 %collective-permute-start.3 = (f32[57344]{0:T(1024)S(1)}, f32[57344]{0:T(1024)S(1)}, u32[]{:S(2)}, u32[]{:S(2)}) collective-permute-start(f32[57344]{0:T(1024)S(1)} %constant_dynamic-update-slice_fusion), channel_id=1, source_target_pairs={{0,1},{1,0},{2,3},{3,2},{4,5},{5,4},{6,7},{7,6},{8,9},{9,8},{10,11... | collective-permute-start | bytes 688136 | tf_op jit(solution)/shard_map/ppermute | solution.py:565

commit v3 on v2

--- a/solution.py
+++ b/solution.py
@@ -12,6 +12,7 @@
 PAD = 8
 BATCH = 32
 SLOTS = 16
+PAIRS = SLOTS // 2
 ROWS = 128
 LANES = 128
 PLANE = ROWS + 2 * PAD
@@ -45,7 +46,6 @@
         copy.start()
     lane = lax.broadcasted_iota(I32, (1, LANES), 1)
     record = jnp.where(lane == 0, source_ref[0], jnp.where(lane == 1, duration_ref[0], count_ref[0]))
-    record = jnp.where(lane == 3, lax.axis_index("rel"), record)
     for copy in copies:
         copy.wait()
     out_ref[pl.ds(rows, 1), pl.ds(0, NSENS)] = sensors[...].astype(F32)
@@ -92,13 +92,19 @@
     table,
     gathered,
     scattered,
+    seed_rows,
+    sensor_ints,
+    sensor_reals,
+    flats,
+    patch_seeds,
     scalars,
     sem,
 ):
     blocks = len(order)
     block = first_ref.shape[0] // (blocks // 2)
     me = lax.axis_index("rel")
-    groups = -(-blocks // SLOTS)
+    half = blocks // 2
+    groups = -(-half // PAIRS)
     lane = lax.broadcasted_iota(I32, (8, LANES), 1)
     sub = lax.broadcasted_iota(I32, (8, LANES), 0)
 
@@ -113,27 +119,13 @@
         else:
             place = owner * rows + 8
         par[pl.ds(place, rows), :] = ref[pl.ds(at, rows), :]
-        sens_rows[pl.ds(owner, 1), :] = ref[pl.ds(at + rows, 1), :]
-        meta_rows[pl.ds(owner, 1), :] = ref[pl.ds(at + rows + 1, 1), :]
-
-    half = blocks // 2
+        stand = (owner // SLOTS) * PAIRS + owner % PAIRS + ((owner // PAIRS) % 2) * half
+        sens_rows[pl.ds(stand, 1), :] = ref[pl.ds(at + rows, 1), :]
+        meta_rows[pl.ds(stand, 1), :] = ref[pl.ds(at + rows + 1, 1), :]
+
     wide = lax.broadcasted_iota(I32, (blocks, LANES), 1)
     place = lax.broadcasted_iota(I32, (blocks, LANES), 0)
-    counts = jnp.broadcast_to(meta_rows[:, 2:3], (blocks, LANES))
-    across = jnp.broadcast_to(counts.T[0:1, :], (blocks, blocks))
-    down, left, top = counts[:, :blocks], wide[:, :blocks], place[:, :blocks]
-    ahead = (down > across) | ((down == across) & (top < left))
-    rank = jnp.sum(ahead.astype(F32), axis=0, keepdims=True)
-    wanted = jnp.where(top < half, 2 * top, 2 * (top - half) + 1).astype(F32)
-    order_by = (jnp.broadcast_to(rank, (blocks, blocks)) == wanted).astype(F32)
-    at_least = jnp.sum((counts >= (wide - 8).astype(F32)).astype(F32), axis=0, keepdims=True)
-    sorted_rows = jnp.dot(
-        order_by,
-        jnp.concatenate([sens_rows[...], meta_rows[...]], axis=1),
-        precision=lax.Precision.HIGHEST,
-        preferred_element_type=F32,
-    )
-    sorted_sens, meta = sorted_rows[:, :LANES], jnp.round(sorted_rows[:, LANES:]).astype(I32)
+    meta = meta_rows[...].astype(I32)
 
     pair_lane, pair_row = wide[:half], place[:half]
     first = pair_lane < NSENS
@@ -144,10 +136,11 @@
     def spread(value):
         return jnp.broadcast_to(value, (blocks, LANES))
 
-    turned = pltpu.roll(sorted_sens, NSENS, 1)
-    sens = jnp.round(jnp.where(first, sorted_sens[:half], turned[half:])).astype(I32)
-    watched = jnp.where(first, turned[:half], sorted_sens[half:])
-    source, count, owner_of = spread(meta[:, 0:1]), spread(meta[:, 2:3]), spread(meta[:, 3:4])
+    straight = sens_rows[...]
+    turned = pltpu.roll(straight, NSENS, 1)
+    sens = jnp.where(first, straight[:half], turned[half:]).astype(I32)
+    watched = jnp.where(first, turned[:half], straight[half:])
+    source, count = spread(meta[:, 0:1]), spread(meta[:, 2:3])
     left_x = (((source >> 8) & 255) >> 1) - 3
     left_y = ((source & 255) >> 1) - 3
     fine_x, fine_y = (sens >> 8) & 255, sens & 255
@@ -155,22 +148,23 @@
     cell_x, cell_y = fine_x >> 1, fine_y >> 1
     off_x, off_y = cell_x - paired(left_x), cell_y - paired(left_y)
     inside = (off_x >= 0) & (off_x < 8) & (off_y >= 0) & (off_y < 8)
-    slot_of = (2 * pair_row + jnp.where(first, 0, 1)) % SLOTS
+    slot_of = pair_row % PAIRS + jnp.where(first, 0, PAIRS)
     patch_row = jnp.where(inside, plane * 8 + off_x, -1)
     patch_lane = jnp.where(inside, slot_of * 8 + off_y, -1)
     address = plane * PLANE + PAD + cell_x
-    mine_of = paired(owner_of) == me
-    for at, value in ((4, left_x), (5, left_y), (6, spread(meta[:, 0:1]))):
+    for at, value in ((4, left_x), (5, left_y)):
         meta = jnp.where(wide == at, value, meta)
-    meta = jnp.where(wide >= 8, jnp.broadcast_to(at_least, (blocks, LANES)).astype(I32), meta)
     table[pl.ds(0, half), :] = address + (paired(count) - 1) * FIELD
-    table[pl.ds(half, half), :] = address
-    table[pl.ds(blocks, blocks), :] = meta
+    table[pl.ds(half, blocks), :] = meta
     copy = pltpu.make_async_copy(table, scalars, sem)
     copy.start()
+    sensor_reals[pl.ds(0, half), :] = watched
+    sensor_reals[pl.ds(half, half), :] = ((pair_row // PAIRS) * SLOTS + slot_of == me).astype(F32)
+    for i, value in enumerate((cell_y, patch_lane, patch_row, address)):
+        sensor_ints[pl.ds(i * half, half), :] = value
 
     def about(j, lane_at):
-        return scalars[blocks + (j % 2) * half + j // 2, lane_at]
+        return scalars[half + (j // SLOTS) * PAIRS + j % PAIRS + (j // PAIRS % 2) * half, lane_at]
 
     names = ("centre", "east", "west", "north", "south", "diff", "south0", "north1", "northr", "southl", "wx", "wy", "fx", "fy")
     index = {name: i for i, name in enumerate(names)}
@@ -195,7 +189,7 @@
             wx=wx, wy=wy, fx=0.08 * (1.0 - t1 * t1), fy=0.08 * (1.0 - t2 * t2),
         )
 
-    @loop(0, ROWS // 8, unroll=4)
+    @loop(0, ROWS // 8, unroll=16)
     def _(i, carry):
         x = pl.multiple_of(i * 8, 8)
         for z in range(2):
@@ -210,7 +204,7 @@
         return carry
 
     for p in range(8):
-        for ref, fields in ((hist, STEPS), (lam_a, 1), (lam_b, 1)):
+        for ref, fields in ((hist, STEPS), (seed_rows, STEPS), (lam_a, 1), (lam_b, 1)):
             for f in range(fields):
                 ref[pl.ds(f * FIELD + p * PLANE, 8), :] = zeros
                 ref[pl.ds(f * FIELD + p * PLANE + PAD + ROWS, 8), :] = zeros
@@ -249,20 +243,10 @@
                             along_y[py] + k["diff"] * own[1 - z][px][py]
                         )
                         dst[pl.ds(dst_base + plane_at(z, px, py) + x, 8), :] = new
+                        seed_rows[pl.ds(dst_base + plane_at(z, px, py) + x, 8), :] = zeros
             return carry
 
-    forward(planes_ref, 0, hist, 0)
-    for t in range(1, STEPS):
-        forward(hist, (t - 1) * FIELD, hist, t * FIELD)
-
     copy.wait()
-
-    @loop(0, half)
-    def _(j, carry):
-        to = pl.multiple_of(j * LANES, LANES)
-        for s in range(LANES):
-            gathered[pl.ds(to + s, 1), :] = hist[pl.ds(scalars[j, s], 1), :]
-        return carry
 
     slot = lane >> 3
     patches = []
@@ -292,9 +276,11 @@
             ks.append({name: jnp.where(valid, value, 0.0) for name, value in made.items()})
         spot = (sub == 3) & ((lane & 7) == 3)
         state = [[[zeros for _ in range(2)] for _ in range(2)] for _ in range(2)]
-        plume = []
-        for t in range(STEPS):
-            plume.append(state)
+        patches.append((ks, valid, lasts, of_plane, emits, spot, [state]))
+
+    def plume_forward(t):
+        for ks, _, lasts, of_plane, emits, spot, plume in patches:
+            state = plume[t]
             new = [[[None, None], [None, None]], [[None, None], [None, None]]]
             for z in range(2):
                 k = ks[z]
@@ -314,11 +300,14 @@
                         emit = spot & (of_plane == z * 4 + px * 2 + py) & (t < emits)
                         value = value + jnp.where(emit, 4.0, 0.0)
                         new[z][px][py] = jnp.where(t < lasts, value, c)
-            state = new
-        patches.append((ks, valid, lasts, plume, state))
-
-    def row_of(value, j):
-        return jnp.broadcast_to(value[j : j + 1, :], (LANES, LANES))
+            plume.append(new)
+
+    for t in range(STEPS):
+        plume_forward(t)
+        if t == 0:
+            forward(planes_ref, 0, hist, 0)
+        else:
+            forward(hist, (t - 1) * FIELD, hist, t * FIELD)
 
     def with_rows(a, b):
         return lax.dot_general(a, b, (((1,), (1,)), ((), ())), preferred_element_type=F32)
@@ -327,57 +316,62 @@
     lane_sq = lax.broadcasted_iota(I32, (LANES, LANES), 1)
     diagonal = sub_sq == lane_sq
     batch = (lane_sq // BATCH) == (sub_sq // BATCH)
-    row_id = address.astype(F32)
-    row_down = row_id.T
-    loss = jnp.zeros((1, LANES), F32)
+    for g in range(groups):
+        final = patches[g][-1][STEPS]
+        flat = jnp.concatenate([final[z][px][py] for z in range(2) for px in range(2) for py in range(2)], axis=0)
+        flats[pl.ds(g * LANES, LANES), :] = jnp.concatenate(split(flat), axis=0)
+        patch_seeds[pl.ds(g * LANES, LANES), :] = jnp.zeros((LANES, LANES), F32)
+    misfit_row = sensor_reals.at[pl.ds(2 * half, 1), :]
+    misfit_row[...] = jnp.zeros((1, LANES), F32)
+
+    @loop(0, half, unroll=PAIRS)
+    def _(j, carry):
+        to = pl.multiple_of(j * LANES, LANES)
+        group = pl.ds(pl.multiple_of(j // PAIRS * LANES, LANES), LANES)
+        for s in range(LANES):
+            gathered[pl.ds(to + s, 1), :] = hist[pl.ds(scalars[j, s], 1), :]
+
+        def row_of(i):
+            return jnp.broadcast_to(sensor_ints[pl.ds(i * half + j, 1), :], (LANES, LANES))
+
+        at_lane = (sub_sq == row_of(0)).astype(F32).astype(BF16)
+        at_patch = (sub_sq == row_of(1)).astype(F32).astype(BF16)
+        put = sub_sq[:NSENS] == row_of(2)[:NSENS]
+        high, low = split(gathered[pl.ds(to, LANES), :])
+        far = jnp.dot(high, at_lane, preferred_element_type=F32) + jnp.dot(low, at_lane, preferred_element_type=F32)
+        far = jnp.sum(jnp.where(diagonal, far, 0.0), axis=0, keepdims=True)
+        near = jnp.dot(flats[group, :], at_patch, preferred_element_type=F32)
+        near = jnp.sum(jnp.where(put, near[:NSENS] + near[NSENS:], 0.0), axis=0, keepdims=True)
+        residual = far + near - sensor_reals[pl.ds(j, 1), :]
+        misfit_row[...] += sensor_reals[pl.ds(half + j, 1), :] * residual * residual
+        row_id = row_of(3).astype(F32)
+        same = (row_id == row_id.T) & batch
+        high, low = split(jnp.where(same, jnp.broadcast_to(residual, (LANES, LANES)), 0.0))
+        scattered[pl.ds(to, LANES), :] = with_rows(high, at_lane) + with_rows(low, at_lane)
+        put = jnp.where(put, jnp.broadcast_to(residual, (NSENS, LANES)), 0.0)
+        patch_seeds[group, :] += with_rows(jnp.concatenate(split(put), axis=0), at_patch)
+        for part in range(0, LANES, BATCH):
+            spots = [pl.ds(scalars[j, s], 1) for s in range(part, part + BATCH)]
+            news = [seed_rows[spot, :] + scattered[pl.ds(to + part + s, 1), :] for s, spot in enumerate(spots)]
+            for spot, new in zip(spots, news):
+                seed_rows[spot, :] = new
+
     seeds = []
     for g in range(groups):
-        final = patches[g][4]
-        flat = jnp.concatenate([final[z][px][py] for z in range(2) for px in range(2) for py in range(2)], axis=0)
-        flat = jnp.concatenate(split(flat), axis=0)
-        seed = jnp.zeros((LANES, LANES), F32)
-        for j in range(g * SLOTS // 2, min(half, (g + 1) * SLOTS // 2)):
-            at_lane = (sub_sq == row_of(cell_y, j)).astype(F32).astype(BF16)
-            at_patch = (sub_sq == row_of(patch_lane, j)).astype(F32).astype(BF16)
-            put = sub_sq[:NSENS] == row_of(patch_row, j)[:NSENS]
-            high, low = split(gathered[pl.ds(j * LANES, LANES), :])
-            far = jnp.dot(high, at_lane, preferred_element_type=F32) + jnp.dot(low, at_lane, preferred_element_type=F32)
-            far = jnp.sum(jnp.where(diagonal, far, 0.0), axis=0, keepdims=True)
-            near = jnp.dot(flat, at_patch, preferred_element_type=F32)
-            near = jnp.sum(jnp.where(put, near[:NSENS] + near[NSENS:], 0.0), axis=0, keepdims=True)
-            residual = far + near - watched[j : j + 1, :]
-            loss = loss + jnp.where(mine_of[j : j + 1, :], residual * residual, 0.0)
-            same = (jnp.broadcast_to(row_down[:, j : j + 1], (LANES, LANES)) == row_of(row_id, j)) & batch
-            high, low = split(jnp.where(same, jnp.broadcast_to(residual, (LANES, LANES)), 0.0))
-            scattered[pl.ds(j * LANES, LANES), :] = with_rows(high, at_lane) + with_rows(low, at_lane)
-            put = jnp.where(put, jnp.broadcast_to(residual, (NSENS, LANES)), 0.0)
-            seed = seed + with_rows(jnp.concatenate(split(put), axis=0), at_patch)
-        seed = seed[:NSENS] + seed[NSENS:]
+        seed = patch_seeds[pl.ds(g * LANES, NSENS), :] + patch_seeds[pl.ds(g * LANES + NSENS, NSENS), :]
         seeds.append(
             [[[seed[((z * 2 + px) * 2 + py) * 8 :][:8] for py in range(2)] for px in range(2)] for z in range(2)]
         )
-    misfit_ref[0] = jnp.sum(loss) * (0.5 / NSENS)
-
-    def seed_sensors(ref, t):
-        @loop(scalars[blocks, 8 + t + 1], scalars[blocks, 8 + t])
-        def _(j, carry):
-            row, column = j // 2, (j % 2) * NSENS
-            at = pl.multiple_of(j * NSENS, NSENS)
-            for part in range(0, NSENS, BATCH):
-                spots = [pl.ds(scalars[half + row, column + s], 1) for s in range(part, part + BATCH)]
-                news = [ref[spot, :] + scattered[pl.ds(at + part + s, 1), :] for s, spot in enumerate(spots)]
-                for spot, new in zip(spots, news):
-                    ref[spot, :] = new
-            return carry
+    misfit_ref[0] = jnp.sum(misfit_row[...]) * (0.5 / NSENS)
 
     def acc_at(q, z, x):
         return pl.ds((q * 2 + z) * ROWS + x, 8)
 
-    def backward(src, dst, conc, conc_base, first, last):
+    def backward(src, src_base, dst, seed_base, conc, conc_base, first, last):
         @loop(0, ROWS // 8, unroll=16)
         def _(i, carry):
             x = pl.multiple_of(i * 8, 8)
-            lam, lam_odd, lam_even = load(src, 0, x)
+            lam, lam_odd, lam_even = load(src, src_base, x)
             own, odd, even = load(conc, conc_base, x)
             diffs = [coef[coef_at("diff", z, x), :] for z in range(2)]
             for z in range(2):
@@ -401,7 +395,8 @@
                             new = (k["centre"] * lam[z][px][py] + along_x) + (
                                 along_y[py] + diffs[1 - z] * lam[1 - z][px][py]
                             )
-                            dst[pl.ds(plane_at(z, px, py) + x, 8), :] = new
+                            spot = plane_at(z, px, py) + x
+                            dst[pl.ds(spot, 8), :] = new + seed_rows[pl.ds(seed_base + spot, 8), :]
                 sums = [None] * 5
                 for px in range(2):
                     c0, c1 = own[z][px]
@@ -424,50 +419,19 @@
                     acc[at, :] = sums[q] if first else acc[at, :] + sums[q]
             return carry
 
-    @loop(0, FIELD // 64)
-    def _(i, carry):
-        lam_a[pl.ds(pl.multiple_of(i * 64, 64), 64), :] = jnp.zeros((64, LANES), F32)
-        return carry
-
-    src, dst = lam_a, lam_b
-    for t in range(STEPS - 1, -1, -1):
-        seed_sensors(src, t + 1)
-        if t == 0:
-            backward(src, dst, planes_ref, 0, False, True)
-        else:
-            backward(src, dst, hist, (t - 1) * FIELD, t == STEPS - 1, False)
-        src, dst = dst, src
-
-    def chain(sums, diff, wx, wy, fx, fy):
-        to_east, to_west, to_north, to_south, rise = sums
-
-        def wind(w, up, down, factor):
-            plus = jnp.where(w > 0.0, 1.0, jnp.where(w == 0.0, 0.5, 0.0))
-            return -(plus * up + (1.0 - plus) * down) * factor
-
-        g0 = (to_east - to_west + to_north - to_south + rise) * diff
-        return g0, wind(wx, to_west, to_east, fx), wind(wy, to_south, to_north, fy)
-
-    @loop(0, ROWS // 8, unroll=16)
-    def _(i, carry):
-        x = pl.multiple_of(i * 8, 8)
-        for z in range(2):
-            sums = [acc[acc_at(q, z, x), :] for q in range(5)]
-            made = chain(sums, *(coef[coef_at(name, z, x), :] for name in ("diff", "wx", "wy", "fx", "fy")))
-            for f in range(3):
-                grad[pl.ds((f * 2 + z) * ROWS + 8 + x, 8), :] = made[f]
-        return carry
-
-    for g in range(groups):
-        members = range(g * SLOTS, min(blocks, (g + 1) * SLOTS))
-        ks, valid, lasts, plume, _ = patches[g]
-        seed = seeds[g]
-        lam = [
-            [[jnp.where(lasts == STEPS, seed[z][px][py], 0.0) for py in range(2)] for px in range(2)] for z in range(2)
+    lams = [
+        [
+            [[jnp.where(patch[2] == STEPS, seed[z][px][py], 0.0) for py in range(2)] for px in range(2)]
+            for z in range(2)
         ]
-        sums = [[zeros] * 5 for _ in range(2)]
-        for t in range(STEPS - 1, 0, -1):
-            state = plume[t]
+        for patch, seed in zip(patches, seeds)
+    ]
+    plume_sums = [[[zeros] * 5 for _ in range(2)] for _ in range(groups)]
+
+    def plume_backward(t):
+        for g in range(groups):
+            ks, _, lasts, _, _, _, plume = patches[g]
+            state, lam, seed, sums = plume[t], lams[g], seeds[g], plume_sums[g]
             new = [[[None, None], [None, None]], [[None, None], [None, None]]]
             for z in range(2):
                 k = ks[z]
@@ -493,7 +457,40 @@
                             sums[z][q] = sums[z][q] + l * d
                         value = (k["centre"] * l + along_x) + (along_y + ks[1 - z]["diff"] * lam[1 - z][px][py])
                         new[z][px][py] = value + jnp.where(lasts == t, seed[z][px][py], 0.0)
-            lam = new
+            lams[g] = new
+    src, dst, src_base = seed_rows, lam_b, (STEPS - 1) * FIELD
+    for t in range(STEPS - 1, -1, -1):
+        if t == 0:
+            backward(src, src_base, dst, 0, planes_ref, 0, False, True)
+        else:
+            backward(src, src_base, dst, (t - 1) * FIELD, hist, (t - 1) * FIELD, t == STEPS - 1, False)
+            plume_backward(t)
+        src, dst, src_base = dst, (lam_a if dst is lam_b else lam_b), 0
+
+    def chain(sums, diff, wx, wy, fx, fy):
+        to_east, to_west, to_north, to_south, rise = sums
+
+        def wind(w, up, down, factor):
+            plus = jnp.where(w > 0.0, 1.0, jnp.where(w == 0.0, 0.5, 0.0))
+            return -(plus * up + (1.0 - plus) * down) * factor
+
+        g0 = (to_east - to_west + to_north - to_south + rise) * diff
+        return g0, wind(wx, to_west, to_east, fx), wind(wy, to_south, to_north, fy)
+
+    @loop(0, ROWS // 8, unroll=16)
+    def _(i, carry):
+        x = pl.multiple_of(i * 8, 8)
+        for z in range(2):
+            sums = [acc[acc_at(q, z, x), :] for q in range(5)]
+            made = chain(sums, *(coef[coef_at(name, z, x), :] for name in ("diff", "wx", "wy", "fx", "fy")))
+            for f in range(3):
+                grad[pl.ds((f * 2 + z) * ROWS + 8 + x, 8), :] = made[f]
+        return carry
+
+    for g in range(groups):
+        members = range(g * SLOTS, min(blocks, (g + 1) * SLOTS))
+        ks, valid = patches[g][:2]
+        sums = plume_sums[g]
         made = []
         for z in range(2):
             k = ks[z]
@@ -581,10 +578,15 @@
                 pltpu.VMEM((6 * ROWS + 16, LANES), F32),
                 pltpu.VMEM((size, LANES), F32),
                 pltpu.VMEM((size, LANES), F32),
-                pltpu.VMEM((2 * size, LANES), I32),
+                pltpu.VMEM((size // 2 + size, LANES), I32),
                 pltpu.VMEM((size * NSENS, LANES), F32),
                 pltpu.VMEM((size * NSENS, LANES), F32),
-                pltpu.SMEM((2 * size, LANES), I32),
+                pltpu.VMEM((STEPS * FIELD, LANES), F32),
+                pltpu.VMEM((2 * size, LANES), I32),
+                pltpu.VMEM((size + 8, LANES), F32),
+                pltpu.VMEM((-(-size // SLOTS) * LANES, LANES), BF16),
+                pltpu.VMEM((-(-size // SLOTS) * LANES, LANES), F32),
+                pltpu.SMEM((size // 2 + size, LANES), I32),
                 pltpu.SemaphoreType.DMA,
             ],
             compiler_params=pltpu.CompilerParams(vmem_limit_bytes=VMEM_LIMIT),

time: 32.5 us -> 29.9 us (0.920)
  Pallas kernels: 13.9 us -> 11.3 us
    pallas_call x1, Pallas kernels: 12.3 us -> 9.72 us  [local(): pl.pallas_call(functools.partial(gradient_kernel, order, rows), out_shape...]
where the time goes in v3:
time: 29.9 us; the launch traced here: 29.7 us
  Pallas kernels  11.3 us (38%)
  starting transfers between devices  8.04 us (27%)
  waiting for transfers between devices  7.71 us (26%)
  between operations  2.62 us (9%)
    pallas_call x1, Pallas kernels, local(): pl.pallas_call(functools.partial(gradient_kernel, order, rows), out_shape...  9.72 us
    ppermute x4, starting transfers between devices, local(): got = lax.ppermute(held, 'rel', [(i, i ^ bit) for i in range(size)])  8.04 us
    ppermute x4, waiting for transfers between devices, local(): got = lax.ppermute(held, 'rel', [(i, i ^ bit) for i in range(size)])  7.71 us
    pallas_call x1, Pallas kernels, local(): pl.pallas_call(pack_kernel, out_shape=pltpu.VMEM((block, LANES), F32), in...  0.89 us
    pallas_call x1, Pallas kernels, local(): pl.pallas_call(planes_kernel, out_shape=jax.ShapeDtypeStruct((FIELD, LANE...  0.65 us
  transfers between devices with their start and end apart: 4, of which 4 were waited for; matrix products, arithmetic and copies ran while one was open for 0% of the time, Pallas kernels for 2%

profile of v3, /device:TPU:0, one launch (start us, length us, event | category | flops | bytes accessed | tf_op | source)
XLA Modules:
  0.0 29.7 jit_solution(9546576093735983520)
XLA Ops:
  2.6 0.0 copy-start
  2.6 0.9 %shard_map.86 = f32[56,128]{1,0:T(8,128)S(1)} custom-call(s32[1]{0:T(128)S(6)} %copy.12.source_ref, s32[1]{0:T(128)S(6)} %copy.13.duration_ref, s32[1]{0:T(128)S(6)} %copy.14.count_ref, f32[48,128]{1,0:T(8,128)} %bitcast.9, s32[1,64]{1,0:T(1,128)} %sensors_ref.1, f32[1,64]{1,0:T(1,128)} %observed_ref.1), custom_call_target="tpu_custom_call" | custom-call | tf_op jit(solution)/shard_map/pallas_call | solution.py:541
  3.5 3.1 %collective-permute-start = (f32[7168]{0:T(1024)S(1)}, f32[7168]{0:T(1024)S(1)}, u32[]{:S(2)}, u32[]{:S(2)}) collective-permute-start(f32[7168]{0:T(1024)S(1)} %bitcast.7), channel_id=1, source_target_pairs={{0,4},{1,5},{2,6},{3,7},{4,0},{5,1},{6,2},{7,3},{8,12},{9,13},{10,... | collective-permute-start | bytes 86024 | tf_op jit(solution)/shard_map/ppermute | solution.py:562
  6.6 1.8 %collective-permute-done = f32[7168]{0:T(1024)S(1)} collective-permute-done((f32[7168]{0:T(1024)S(1)}, f32[7168]{0:T(1024)S(1)}, u32[]{:S(2)}, u32[]{:S(2)}) %collective-permute-start) | collective-permute-done | bytes 28704 | tf_op jit(solution)/shard_map/ppermute | solution.py:562
  8.4 3.0 %collective-permute-start.1 = (f32[14336]{0:T(1024)S(1)}, f32[14336]{0:T(1024)S(1)}, u32[]{:S(2)}, u32[]{:S(2)}) collective-permute-start(f32[14336]{0:T(1024)S(1)} %constant_dynamic-update-slice_fusion.2), channel_id=1, source_target_pairs={{0,8},{1,9},{2,10},{3,11},{4,12},{5,13},{6,14},{7,15},{8,0},{9,1},... | collective-permute-start | bytes 172040 | tf_op jit(solution)/shard_map/ppermute | solution.py:562
  11.5 2.1 %collective-permute-done.1 = f32[14336]{0:T(1024)S(1)} collective-permute-done((f32[14336]{0:T(1024)S(1)}, f32[14336]{0:T(1024)S(1)}, u32[]{:S(2)}, u32[]{:S(2)}) %collective-permute-start.1) | collective-permute-done | bytes 57376 | tf_op jit(solution)/shard_map/ppermute | solution.py:562
  13.6 1.9 %collective-permute-start.2 = (f32[28672]{0:T(1024)S(1)}, f32[28672]{0:T(1024)S(1)}, u32[]{:S(2)}, u32[]{:S(2)}) collective-permute-start(f32[28672]{0:T(1024)S(1)} %constant_dynamic-update-slice_fusion.1), channel_id=1, source_target_pairs={{0,2},{1,3},{2,0},{3,1},{4,6},{5,7},{6,4},{7,5},{8,10},{9,11},{10,... | collective-permute-start | bytes 344072 | tf_op jit(solution)/shard_map/ppermute | solution.py:562
  15.5 2.9 %collective-permute-done.2 = f32[28672]{0:T(1024)S(1)} collective-permute-done((f32[28672]{0:T(1024)S(1)}, f32[28672]{0:T(1024)S(1)}, u32[]{:S(2)}, u32[]{:S(2)}) %collective-permute-start.2) | collective-permute-done | bytes 114720 | tf_op jit(solution)/shard_map/ppermute | solution.py:562
  18.4 0.1 collective-permute-start.3
  18.5 0.0 copy-done
  18.5 0.7 %shard_map.87.planes_ref = f32[1152,128]{1,0:T(8,128)S(1)} custom-call(f32[2,256,256]{2,1,0:T(8,128)S(1)} %copy-done), custom_call_target="tpu_custom_call" | custom-call | tf_op jit(solution)/shard_map/pallas_call | solution.py:552
  19.2 0.8 %collective-permute-done.3 = f32[57344]{0:T(1024)S(1)} collective-permute-done((f32[57344]{0:T(1024)S(1)}, f32[57344]{0:T(1024)S(1)}, u32[]{:S(2)}, u32[]{:S(2)}) %collective-permute-start.3) | collective-permute-done | bytes 229408 | tf_op jit(solution)/shard_map/ppermute | solution.py:562
  20.0 9.7 %shard_map.88 = (f32[48,128]{1,0:T(8,128)}, f32[1]{0:T(128)}) custom-call(f32[448,128]{1,0:T(8,128)S(1)} %bitcast.5, f32[448,128]{1,0:T(8,128)S(1)} %bitcast.6, f32[1152,128]{1,0:T(8,128)S(1)} %shard_map.87.planes_ref), custom_call_target="tpu_custom_call" | custom-call | tf_op jit(solution)/shard_map/pallas_call | solution.py:566
  (6 shorter events, 0.0 us)
Async XLA Ops:
  2.6 15.9 %copy-start = (f32[2,256,256]{2,1,0:T(8,128)S(1)}, f32[2,256,256]{2,1,0:T(8,128)}, u32[]{:S(2)}) copy-start(f32[2,256,256]{2,1,0:T(8,128)} %background_ref.1) | copy-start | bytes 1572868
  3.5 4.9 %collective-permute-start = (f32[7168]{0:T(1024)S(1)}, f32[7168]{0:T(1024)S(1)}, u32[]{:S(2)}, u32[]{:S(2)}) collective-permute-start(f32[7168]{0:T(1024)S(1)} %bitcast.7), channel_id=1, source_target_pairs={{0,4},{1,5},{2,6},{3,7},{4,0},{5,1},{6,2},{7,3},{8,12},{9,13},{10,... | collective-permute-start | bytes 86024 | tf_op jit(solution)/shard_map/ppermute | solution.py:562
  8.4 5.2 %collective-permute-start.1 = (f32[14336]{0:T(1024)S(1)}, f32[14336]{0:T(1024)S(1)}, u32[]{:S(2)}, u32[]{:S(2)}) collective-permute-start(f32[14336]{0:T(1024)S(1)} %constant_dynamic-update-slice_fusion.2), channel_id=1, source_target_pairs={{0,8},{1,9},{2,10},{3,11},{4,12},{5,13},{6,14},{7,15},{8,0},{9,1},... | collective-permute-start | bytes 172040 | tf_op jit(solution)/shard_map/ppermute | solution.py:562
  13.6 4.8 %collective-permute-start.2 = (f32[28672]{0:T(1024)S(1)}, f32[28672]{0:T(1024)S(1)}, u32[]{:S(2)}, u32[]{:S(2)}) collective-permute-start(f32[28672]{0:T(1024)S(1)} %constant_dynamic-update-slice_fusion.1), channel_id=1, source_target_pairs={{0,2},{1,3},{2,0},{3,1},{4,6},{5,7},{6,4},{7,5},{8,10},{9,11},{10,... | collective-permute-start | bytes 344072 | tf_op jit(solution)/shard_map/ppermute | solution.py:562
  18.4 1.6 %collective-permute-start.3 = (f32[57344]{0:T(1024)S(1)}, f32[57344]{0:T(1024)S(1)}, u32[]{:S(2)}, u32[]{:S(2)}) collective-permute-start(f32[57344]{0:T(1024)S(1)} %constant_dynamic-update-slice_fusion), channel_id=1, source_target_pairs={{0,1},{1,0},{2,3},{3,2},{4,5},{5,4},{6,7},{7,6},{8,9},{9,8},{10,11... | collective-permute-start | bytes 688136 | tf_op jit(solution)/shard_map/ppermute | solution.py:562

commit v4 on v3

--- a/solution.py
+++ b/solution.py
@@ -10,7 +10,7 @@
 STEPS = 6
 NSENS = 64
 PAD = 8
-BATCH = 32
+BATCH = 16
 SLOTS = 16
 PAIRS = SLOTS // 2
 ROWS = 128
@@ -97,6 +97,9 @@
     sensor_reals,
     flats,
     patch_seeds,
+    slope_lap,
+    slope_x,
+    slope_y,
     scalars,
     sem,
 ):
@@ -104,6 +107,7 @@
     block = first_ref.shape[0] // (blocks // 2)
     me = lax.axis_index("rel")
     half = blocks // 2
+    slopes = (slope_lap, slope_x, slope_y)
     groups = -(-half // PAIRS)
     lane = lax.broadcasted_iota(I32, (8, LANES), 1)
     sub = lax.broadcasted_iota(I32, (8, LANES), 0)
@@ -166,7 +170,7 @@
     def about(j, lane_at):
         return scalars[half + (j // SLOTS) * PAIRS + j % PAIRS + (j // PAIRS % 2) * half, lane_at]
 
-    names = ("centre", "east", "west", "north", "south", "diff", "south0", "north1", "northr", "southl", "wx", "wy", "fx", "fy")
+    names = ("centre", "east", "west", "north", "south", "diff", "up_x", "up_y", "northr", "southl", "wx", "wy", "fx", "fy")
     index = {name: i for i, name in enumerate(names)}
 
     def coef_at(name, z, x):
@@ -176,6 +180,9 @@
     for z in range(2):
         coef[coef_at("east", z, -8), :] = zeros
         coef[coef_at("west", z, ROWS), :] = zeros
+
+    def share(w):
+        return jnp.where(w > 0.0, 1.0, jnp.where(w == 0.0, 0.5, 0.0))
 
     def coefficients(p0, p1, p2):
         diff = 0.05 * jnp.exp(p0)
@@ -195,8 +202,7 @@
         for z in range(2):
             p0, p1, p2 = (par[pl.ds((f * 2 + z) * ROWS + 8 + x, 8), :] for f in range(3))
             made = coefficients(p0, p1, p2)
-            made["south0"] = jnp.where(lane == 0, 0.0, made["south"])
-            made["north1"] = jnp.where(lane == LANES - 1, 0.0, made["north"])
+            made["up_x"], made["up_y"] = share(made["wx"]), share(made["wy"])
             made["northr"] = jnp.where(lane == 0, 0.0, pltpu.roll(made["north"], 1, 1))
             made["southl"] = jnp.where(lane == LANES - 1, 0.0, pltpu.roll(made["south"], LANES - 1, 1))
             for name, value in made.items():
@@ -224,27 +230,29 @@
             x = pl.multiple_of(i * 8, 8)
             own, odd, even = load(src, src_base, x)
             for z in range(2):
-                k = {
-                    name: coef[coef_at(name, z, x), :]
-                    for name in ("centre", "east", "west", "north", "south", "diff", "south0", "north1")
-                }
+                k = {name: coef[coef_at(name, z, x), :] for name in ("diff", "wx", "wy", "up_x", "up_y")}
+                to_x, lap_x = [None] * 2, [None] * 2
+                for py in range(2):
+                    c0, c1 = own[z][0][py], own[z][1][py]
+                    mid, east = c1 - c0, even[z][py] - c1
+                    to_x[py] = (mid, east)
+                    lap_x[py] = (mid - (c0 - odd[z][py]), east - mid)
                 for px in range(2):
                     c0, c1 = own[z][px]
-                    along_y = (
-                        k["north"] * c1 + k["south0"] * pltpu.roll(c1, 1, 1),
-                        k["north1"] * pltpu.roll(c0, LANES - 1, 1) + k["south"] * c0,
-                    )
+                    mid = c1 - c0
+                    north = jnp.where(lane == LANES - 1, 0.0, pltpu.roll(c0, LANES - 1, 1)) - c1
+                    south = c0 - jnp.where(lane == 0, 0.0, pltpu.roll(c1, 1, 1))
+                    to_y, lap_y = (mid, north), (mid - south, north - mid)
                     for py in range(2):
-                        if px == 0:
-                            along_x = k["east"] * own[z][1][py] + k["west"] * odd[z][py]
-                        else:
-                            along_x = k["east"] * even[z][py] + k["west"] * own[z][0][py]
-                        new = (k["centre"] * own[z][px][py] + along_x) + (
-                            along_y[py] + k["diff"] * own[1 - z][px][py]
-                        )
-                        dst[pl.ds(dst_base + plane_at(z, px, py) + x, 8), :] = new
-                        seed_rows[pl.ds(dst_base + plane_at(z, px, py) + x, 8), :] = zeros
-            return carry
+                        c = own[z][px][py]
+                        lap = (lap_x[py][px] + lap_y[py]) + ((own[1 - z][px][py] - c) - c)
+                        up_x = to_x[py][px] - k["up_x"] * lap_x[py][px]
+                        up_y = to_y[py] - k["up_y"] * lap_y[py]
+                        at = pl.ds(dst_base + plane_at(z, px, py) + x, 8)
+                        dst[at, :] = (c + k["diff"] * lap) - (k["wx"] * up_x + k["wy"] * up_y)
+                        seed_rows[at, :] = zeros
+                        for ref, value in zip(slopes, (lap, up_x, up_y)):
+                            ref[at, :] = value
 
     copy.wait()
 
@@ -324,37 +332,66 @@
     misfit_row = sensor_reals.at[pl.ds(2 * half, 1), :]
     misfit_row[...] = jnp.zeros((1, LANES), F32)
 
-    @loop(0, half, unroll=PAIRS)
-    def _(j, carry):
+    def read_rows(j, part):
         to = pl.multiple_of(j * LANES, LANES)
-        group = pl.ds(pl.multiple_of(j // PAIRS * LANES, LANES), LANES)
-        for s in range(LANES):
+        for s in range(part * BATCH, (part + 1) * BATCH):
             gathered[pl.ds(to + s, 1), :] = hist[pl.ds(scalars[j, s], 1), :]
 
-        def row_of(i):
-            return jnp.broadcast_to(sensor_ints[pl.ds(i * half + j, 1), :], (LANES, LANES))
-
-        at_lane = (sub_sq == row_of(0)).astype(F32).astype(BF16)
-        at_patch = (sub_sq == row_of(1)).astype(F32).astype(BF16)
-        put = sub_sq[:NSENS] == row_of(2)[:NSENS]
-        high, low = split(gathered[pl.ds(to, LANES), :])
+    def add_rows(j, part):
+        to = pl.multiple_of(j * LANES, LANES)
+        spots = [pl.ds(scalars[j, s], 1) for s in range(part * BATCH, (part + 1) * BATCH)]
+        news = [seed_rows[spot, :] + scattered[pl.ds(to + part * BATCH + s, 1), :] for s, spot in enumerate(spots)]
+        for spot, new in zip(spots, news):
+            seed_rows[spot, :] = new
+
+    def row_of(i, j):
+        return jnp.broadcast_to(sensor_ints[pl.ds(i * half + j, 1), :], (LANES, LANES))
+
+    def group_of(j):
+        return pl.ds(pl.multiple_of(j // PAIRS * LANES, LANES), LANES)
+
+    def values_of(j):
+        at_lane = (sub_sq == row_of(0, j)).astype(F32).astype(BF16)
+        at_patch = (sub_sq == row_of(1, j)).astype(F32).astype(BF16)
+        put = sub_sq[:NSENS] == row_of(2, j)[:NSENS]
+        high, low = split(gathered[pl.ds(pl.multiple_of(j * LANES, LANES), LANES), :])
         far = jnp.dot(high, at_lane, preferred_element_type=F32) + jnp.dot(low, at_lane, preferred_element_type=F32)
+        near = jnp.dot(flats[group_of(j), :], at_patch, preferred_element_type=F32)
+        return at_lane, at_patch, put, far, near
+
+    def residuals_of(j, at_lane, at_patch, put, far, near):
         far = jnp.sum(jnp.where(diagonal, far, 0.0), axis=0, keepdims=True)
-        near = jnp.dot(flats[group, :], at_patch, preferred_element_type=F32)
         near = jnp.sum(jnp.where(put, near[:NSENS] + near[NSENS:], 0.0), axis=0, keepdims=True)
         residual = far + near - sensor_reals[pl.ds(j, 1), :]
         misfit_row[...] += sensor_reals[pl.ds(half + j, 1), :] * residual * residual
-        row_id = row_of(3).astype(F32)
+        row_id = row_of(3, j).astype(F32)
         same = (row_id == row_id.T) & batch
+        return residual, same, at_lane, at_patch, put
+
+    def seeds_of(j, residual, same, at_lane, at_patch, put):
         high, low = split(jnp.where(same, jnp.broadcast_to(residual, (LANES, LANES)), 0.0))
+        to = pl.multiple_of(j * LANES, LANES)
         scattered[pl.ds(to, LANES), :] = with_rows(high, at_lane) + with_rows(low, at_lane)
         put = jnp.where(put, jnp.broadcast_to(residual, (NSENS, LANES)), 0.0)
-        patch_seeds[group, :] += with_rows(jnp.concatenate(split(put), axis=0), at_patch)
-        for part in range(0, LANES, BATCH):
-            spots = [pl.ds(scalars[j, s], 1) for s in range(part, part + BATCH)]
-            news = [seed_rows[spot, :] + scattered[pl.ds(to + part + s, 1), :] for s, spot in enumerate(spots)]
-            for spot, new in zip(spots, news):
-                seed_rows[spot, :] = new
+        patch_seeds[group_of(j), :] += with_rows(jnp.concatenate(split(put), axis=0), at_patch)
+
+    @loop(0, groups, unroll=groups == 1)
+    def _(g, carry):
+        made = {}
+        for i in range(PAIRS + 2):
+            for part in range(LANES // BATCH):
+                if i < PAIRS:
+                    read_rows(g * PAIRS + i, part)
+                if i >= 2:
+                    add_rows(g * PAIRS + i - 2, part)
+                if 1 <= i <= PAIRS:
+                    j = g * PAIRS + i - 1
+                    if part == 0:
+                        made[i] = values_of(j)
+                    elif part == 1:
+                        made[i] = residuals_of(j, *made[i])
+                    elif part == 2:
+                        seeds_of(j, *made[i])
 
     seeds = []
     for g in range(groups):
@@ -367,12 +404,11 @@
     def acc_at(q, z, x):
         return pl.ds((q * 2 + z) * ROWS + x, 8)
 
-    def backward(src, src_base, dst, seed_base, conc, conc_base, first, last):
+    def backward(src, src_base, dst, seed_base, slope_base, first, last):
         @loop(0, ROWS // 8, unroll=16)
         def _(i, carry):
             x = pl.multiple_of(i * 8, 8)
             lam, lam_odd, lam_even = load(src, src_base, x)
-            own, odd, even = load(conc, conc_base, x)
             diffs = [coef[coef_at("diff", z, x), :] for z in range(2)]
             for z in range(2):
                 if not last:
@@ -397,27 +433,16 @@
                             )
                             spot = plane_at(z, px, py) + x
                             dst[pl.ds(spot, 8), :] = new + seed_rows[pl.ds(seed_base + spot, 8), :]
-                sums = [None] * 5
+                sums = [None] * 3
                 for px in range(2):
-                    c0, c1 = own[z][px]
-                    mid = c1 - c0
-                    to_north = (mid, jnp.where(lane == LANES - 1, 0.0, pltpu.roll(c0, LANES - 1, 1)) - c1)
-                    to_south = (c0 - jnp.where(lane == 0, 0.0, pltpu.roll(c1, 1, 1)), mid)
                     for py in range(2):
-                        c, l = own[z][px][py], lam[z][px][py]
-                        mid_x = own[z][1][py] - own[z][0][py]
-                        if px == 0:
-                            to_east, to_west = mid_x, c - odd[z][py]
-                        else:
-                            to_east, to_west = even[z][py] - c, mid_x
-                        rise = own[1 - z][px][py] - 2.0 * c
-                        for q, d in enumerate((to_east, to_west, to_north[py], to_south[py], rise)):
-                            term = l * d
+                        at = pl.ds(slope_base + plane_at(z, px, py) + x, 8)
+                        for q, ref in enumerate(slopes):
+                            term = lam[z][px][py] * ref[at, :]
                             sums[q] = term if sums[q] is None else sums[q] + term
-                for q in range(5):
+                for q in range(3):
                     at = acc_at(q, z, x)
                     acc[at, :] = sums[q] if first else acc[at, :] + sums[q]
-            return carry
 
     lams = [
         [
@@ -461,9 +486,9 @@
     src, dst, src_base = seed_rows, lam_b, (STEPS - 1) * FIELD
     for t in range(STEPS - 1, -1, -1):
         if t == 0:
-            backward(src, src_base, dst, 0, planes_ref, 0, False, True)
+            backward(src, src_base, dst, 0, 0, False, True)
         else:
-            backward(src, src_base, dst, (t - 1) * FIELD, hist, (t - 1) * FIELD, t == STEPS - 1, False)
+            backward(src, src_base, dst, (t - 1) * FIELD, t * FIELD, t == STEPS - 1, False)
             plume_backward(t)
         src, dst, src_base = dst, (lam_a if dst is lam_b else lam_b), 0
 
@@ -471,7 +496,7 @@
         to_east, to_west, to_north, to_south, rise = sums
 
         def wind(w, up, down, factor):
-            plus = jnp.where(w > 0.0, 1.0, jnp.where(w == 0.0, 0.5, 0.0))
+            plus = share(w)
             return -(plus * up + (1.0 - plus) * down) * factor
 
         g0 = (to_east - to_west + to_north - to_south + rise) * diff
@@ -481,11 +506,10 @@
     def _(i, carry):
         x = pl.multiple_of(i * 8, 8)
         for z in range(2):
-            sums = [acc[acc_at(q, z, x), :] for q in range(5)]
-            made = chain(sums, *(coef[coef_at(name, z, x), :] for name in ("diff", "wx", "wy", "fx", "fy")))
-            for f in range(3):
-                grad[pl.ds((f * 2 + z) * ROWS + 8 + x, 8), :] = made[f]
-        return carry
+            signed = (("diff", 1.0), ("fx", -1.0), ("fy", -1.0))
+            for f, (name, sign) in enumerate(signed):
+                made = acc[acc_at(f, z, x), :] * (sign * coef[coef_at(name, z, x), :])
+                grad[pl.ds((f * 2 + z) * ROWS + 8 + x, 8), :] = made
 
     for g in range(groups):
         members = range(g * SLOTS, min(blocks, (g + 1) * SLOTS))
@@ -574,7 +598,7 @@
                 pltpu.VMEM((STEPS * FIELD, LANES), F32),
                 pltpu.VMEM((FIELD, LANES), F32),
                 pltpu.VMEM((FIELD, LANES), F32),
-                pltpu.VMEM((10 * ROWS, LANES), F32),
+                pltpu.VMEM((6 * ROWS, LANES), F32),
                 pltpu.VMEM((6 * ROWS + 16, LANES), F32),
                 pltpu.VMEM((size, LANES), F32),
                 pltpu.VMEM((size, LANES), F32),
@@ -586,6 +610,9 @@
                 pltpu.VMEM((size + 8, LANES), F32),
                 pltpu.VMEM((-(-size // SLOTS) * LANES, LANES), BF16),
                 pltpu.VMEM((-(-size // SLOTS) * LANES, LANES), F32),
+                pltpu.VMEM((STEPS * FIELD, LANES), F32),
+                pltpu.VMEM((STEPS * FIELD, LANES), F32),
+                pltpu.VMEM((STEPS * FIELD, LANES), F32),
                 pltpu.SMEM((size // 2 + size, LANES), I32),
                 pltpu.SemaphoreType.DMA,
             ],

time: 29.9 us -> 29.7 us (level)
  no operation moved by 1% of the time
where the time goes in v4:
time: 29.7 us; the launch traced here: 29.5 us
  Pallas kernels  11.1 us (37%)
  starting transfers between devices  8.04 us (27%)
  waiting for transfers between devices  7.71 us (26%)
  between operations  2.62 us (9%)
    pallas_call x1, Pallas kernels, local(): pl.pallas_call(functools.partial(gradient_kernel, order, rows), out_shape...  9.5 us
    ppermute x4, starting transfers between devices, local(): got = lax.ppermute(held, 'rel', [(i, i ^ bit) for i in range(size)])  8.04 us
    ppermute x4, waiting for transfers between devices, local(): got = lax.ppermute(held, 'rel', [(i, i ^ bit) for i in range(size)])  7.71 us
    pallas_call x1, Pallas kernels, local(): pl.pallas_call(pack_kernel, out_shape=pltpu.VMEM((block, LANES), F32), in...  0.89 us
    pallas_call x1, Pallas kernels, local(): pl.pallas_call(planes_kernel, out_shape=jax.ShapeDtypeStruct((FIELD, LANE...  0.65 us
  transfers between devices with their start and end apart: 4, of which 4 were waited for; matrix products, arithmetic and copies ran while one was open for 0% of the time, Pallas kernels for 2%

profile of v4, /device:TPU:0, one launch (start us, length us, event | category | flops | bytes accessed | tf_op | source)
XLA Modules:
  0.0 29.5 jit_solution(11404561719548690249)
XLA Ops:
  2.6 0.0 copy-start
  2.6 0.9 %shard_map.86 = f32[56,128]{1,0:T(8,128)S(1)} custom-call(s32[1]{0:T(128)S(6)} %copy.12.source_ref, s32[1]{0:T(128)S(6)} %copy.13.duration_ref, s32[1]{0:T(128)S(6)} %copy.14.count_ref, f32[48,128]{1,0:T(8,128)} %bitcast.9, s32[1,64]{1,0:T(1,128)} %sensors_ref.1, f32[1,64]{1,0:T(1,128)} %observed_ref.1), custom_call_target="tpu_custom_call" | custom-call | tf_op jit(solution)/shard_map/pallas_call | solution.py:565
  3.5 3.1 %collective-permute-start = (f32[7168]{0:T(1024)S(1)}, f32[7168]{0:T(1024)S(1)}, u32[]{:S(2)}, u32[]{:S(2)}) collective-permute-start(f32[7168]{0:T(1024)S(1)} %bitcast.7), channel_id=1, source_target_pairs={{0,4},{1,5},{2,6},{3,7},{4,0},{5,1},{6,2},{7,3},{8,12},{9,13},{10,... | collective-permute-start | bytes 86024 | tf_op jit(solution)/shard_map/ppermute | solution.py:586
  6.6 1.8 %collective-permute-done = f32[7168]{0:T(1024)S(1)} collective-permute-done((f32[7168]{0:T(1024)S(1)}, f32[7168]{0:T(1024)S(1)}, u32[]{:S(2)}, u32[]{:S(2)}) %collective-permute-start) | collective-permute-done | bytes 28704 | tf_op jit(solution)/shard_map/ppermute | solution.py:586
  8.4 3.0 %collective-permute-start.1 = (f32[14336]{0:T(1024)S(1)}, f32[14336]{0:T(1024)S(1)}, u32[]{:S(2)}, u32[]{:S(2)}) collective-permute-start(f32[14336]{0:T(1024)S(1)} %constant_dynamic-update-slice_fusion.2), channel_id=1, source_target_pairs={{0,8},{1,9},{2,10},{3,11},{4,12},{5,13},{6,14},{7,15},{8,0},{9,1},... | collective-permute-start | bytes 172040 | tf_op jit(solution)/shard_map/ppermute | solution.py:586
  11.5 2.1 %collective-permute-done.1 = f32[14336]{0:T(1024)S(1)} collective-permute-done((f32[14336]{0:T(1024)S(1)}, f32[14336]{0:T(1024)S(1)}, u32[]{:S(2)}, u32[]{:S(2)}) %collective-permute-start.1) | collective-permute-done | bytes 57376 | tf_op jit(solution)/shard_map/ppermute | solution.py:586
  13.6 1.9 %collective-permute-start.2 = (f32[28672]{0:T(1024)S(1)}, f32[28672]{0:T(1024)S(1)}, u32[]{:S(2)}, u32[]{:S(2)}) collective-permute-start(f32[28672]{0:T(1024)S(1)} %constant_dynamic-update-slice_fusion.1), channel_id=1, source_target_pairs={{0,2},{1,3},{2,0},{3,1},{4,6},{5,7},{6,4},{7,5},{8,10},{9,11},{10,... | collective-permute-start | bytes 344072 | tf_op jit(solution)/shard_map/ppermute | solution.py:586
  15.5 2.9 %collective-permute-done.2 = f32[28672]{0:T(1024)S(1)} collective-permute-done((f32[28672]{0:T(1024)S(1)}, f32[28672]{0:T(1024)S(1)}, u32[]{:S(2)}, u32[]{:S(2)}) %collective-permute-start.2) | collective-permute-done | bytes 114720 | tf_op jit(solution)/shard_map/ppermute | solution.py:586
  18.4 0.1 collective-permute-start.3
  18.5 0.0 copy-done
  18.5 0.7 %shard_map.87.planes_ref = f32[1152,128]{1,0:T(8,128)S(1)} custom-call(f32[2,256,256]{2,1,0:T(8,128)S(1)} %copy-done), custom_call_target="tpu_custom_call" | custom-call | tf_op jit(solution)/shard_map/pallas_call | solution.py:576
  19.2 0.8 %collective-permute-done.3 = f32[57344]{0:T(1024)S(1)} collective-permute-done((f32[57344]{0:T(1024)S(1)}, f32[57344]{0:T(1024)S(1)}, u32[]{:S(2)}, u32[]{:S(2)}) %collective-permute-start.3) | collective-permute-done | bytes 229408 | tf_op jit(solution)/shard_map/ppermute | solution.py:586
  20.0 9.5 %shard_map.88 = (f32[48,128]{1,0:T(8,128)}, f32[1]{0:T(128)}) custom-call(f32[448,128]{1,0:T(8,128)S(1)} %bitcast.5, f32[448,128]{1,0:T(8,128)S(1)} %bitcast.6, f32[1152,128]{1,0:T(8,128)S(1)} %shard_map.87.planes_ref), custom_call_target="tpu_custom_call" | custom-call | tf_op jit(solution)/shard_map/pallas_call | solution.py:590
  (6 shorter events, 0.0 us)
Async XLA Ops:
  2.6 15.9 %copy-start = (f32[2,256,256]{2,1,0:T(8,128)S(1)}, f32[2,256,256]{2,1,0:T(8,128)}, u32[]{:S(2)}) copy-start(f32[2,256,256]{2,1,0:T(8,128)} %background_ref.1) | copy-start | bytes 1572868
  3.5 4.9 %collective-permute-start = (f32[7168]{0:T(1024)S(1)}, f32[7168]{0:T(1024)S(1)}, u32[]{:S(2)}, u32[]{:S(2)}) collective-permute-start(f32[7168]{0:T(1024)S(1)} %bitcast.7), channel_id=1, source_target_pairs={{0,4},{1,5},{2,6},{3,7},{4,0},{5,1},{6,2},{7,3},{8,12},{9,13},{10,... | collective-permute-start | bytes 86024 | tf_op jit(solution)/shard_map/ppermute | solution.py:586
  8.4 5.2 %collective-permute-start.1 = (f32[14336]{0:T(1024)S(1)}, f32[14336]{0:T(1024)S(1)}, u32[]{:S(2)}, u32[]{:S(2)}) collective-permute-start(f32[14336]{0:T(1024)S(1)} %constant_dynamic-update-slice_fusion.2), channel_id=1, source_target_pairs={{0,8},{1,9},{2,10},{3,11},{4,12},{5,13},{6,14},{7,15},{8,0},{9,1},... | collective-permute-start | bytes 172040 | tf_op jit(solution)/shard_map/ppermute | solution.py:586
  13.6 4.8 %collective-permute-start.2 = (f32[28672]{0:T(1024)S(1)}, f32[28672]{0:T(1024)S(1)}, u32[]{:S(2)}, u32[]{:S(2)}) collective-permute-start(f32[28672]{0:T(1024)S(1)} %constant_dynamic-update-slice_fusion.1), channel_id=1, source_target_pairs={{0,2},{1,3},{2,0},{3,1},{4,6},{5,7},{6,4},{7,5},{8,10},{9,11},{10,... | collective-permute-start | bytes 344072 | tf_op jit(solution)/shard_map/ppermute | solution.py:586
  18.4 1.6 %collective-permute-start.3 = (f32[57344]{0:T(1024)S(1)}, f32[57344]{0:T(1024)S(1)}, u32[]{:S(2)}, u32[]{:S(2)}) collective-permute-start(f32[57344]{0:T(1024)S(1)} %constant_dynamic-update-slice_fusion), channel_id=1, source_target_pairs={{0,1},{1,0},{2,3},{3,2},{4,5},{5,4},{6,7},{7,6},{8,9},{9,8},{10,11... | collective-permute-start | bytes 688136 | tf_op jit(solution)/shard_map/ppermute | solution.py:586
